TPU v7x, 512 devices: a whole 4x8x8 slice. The times are simulated.
512 devices in a mesh: in: 8 (over x, z_lo), out: 8 (over z_hi, core), batch: 8 (over y).
Axes of the slice: x: 4, y: 8, z: 8 (z_hi: 4, z_lo: 2; z = z_hi * 2 + z_lo), core: 2. Of those that a mesh axis runs over, the one named last changes fastest.
Arguments:
- inputs: bfloat16 [2048, 6144], P('batch', 'in'), may hold values from -6 to 6
- out_grad: bfloat16 [2048, 6144], P('batch', 'in'), may hold values from -6 to 6
- pre_act: bfloat16 [2048, 8192], P('batch', 'out'), may hold values from -6 to 6
- w_in: bfloat16 [6144, 8192], P('in', 'out'), may hold values from -0.078125 to 0.078125
- w_out: bfloat16 [8192, 6144], P('out', 'in'), may hold values from -0.0625 to 0.0625
Outputs:
- input_grad: bfloat16 [2048, 6144], P('batch', ('in', 'out'))
- w_in_grad: bfloat16 [6144, 8192], P('in', ('out', 'batch'))
- w_out_grad: bfloat16 [8192, 6144], P('out', ('in', 'batch'))
All inputs are finite; a program needn't handle non-finite values.
Results may differ from a plain program's by a relative error of at most 0.025.
Values may be sent and summed in bfloat16 or wider, within the bound.
No kernel may reach another device: no remote copies, remote signals or barrier semaphores. Data moves between devices by JAX's collectives and lax.ppermute only.
A program may use at most 64 MiB of HBM per device.

v0:
```python
import math

import jax
import jax.numpy as jnp
from jax import lax
from jax.sharding import PartitionSpec as P


def gelu_parts(pre):
    value = pre.astype(jnp.float32)
    cdf = 0.5 * (1.0 + lax.erf(value * 0.7071067811865476))
    density = jnp.exp(-0.5 * value * value) * 0.3989422804014327
    return (value * cdf, cdf + value * density)


def per_device(inputs, out_grad, pre_act, w_in, w_out):
    act_full, deriv_full = gelu_parts(pre_act)
    act = act_full.astype(jnp.bfloat16)
    partial_act = lax.dot_general(
        out_grad, w_out, (((1,), (1,)), ((), ())), preferred_element_type=jnp.float32
    )
    act_grad = lax.psum(partial_act.astype(jnp.bfloat16), "in").astype(jnp.float32)
    pre_grad = (act_grad * deriv_full).astype(jnp.bfloat16)
    input_term = lax.dot_general(
        pre_grad, w_in, (((1,), (1,)), ((), ())), preferred_element_type=jnp.float32
    )
    input_grad = lax.psum_scatter(
        input_term.astype(jnp.bfloat16), "out", scatter_dimension=1, tiled=True
    )
    factor = 1.0 / math.sqrt(inputs.shape[0] * lax.axis_size("batch"))
    w_out_term = (
        lax.dot_general(act, out_grad, (((0,), (0,)), ((), ())), preferred_element_type=jnp.float32)
        * factor
    )
    w_out_grad = lax.psum_scatter(
        w_out_term.astype(jnp.bfloat16), "batch", scatter_dimension=1, tiled=True
    )
    w_in_term = (
        lax.dot_general(
            inputs, pre_grad, (((0,), (0,)), ((), ())), preferred_element_type=jnp.float32
        )
        * factor
    )
    w_in_grad = lax.psum_scatter(
        w_in_term.astype(jnp.bfloat16), "batch", scatter_dimension=1, tiled=True
    )
    return (input_grad, w_in_grad, w_out_grad)


def solution(mesh):
    return jax.shard_map(
        per_device,
        mesh=mesh,
        in_specs=(
            P("batch", "in"),
            P("batch", "in"),
            P("batch", "out"),
            P("in", "out"),
            P("out", "in"),
        ),
        out_specs=(P("batch", ("in", "out")), P("in", ("out", "batch")), P("out", ("in", "batch"))),
        check_vma=False,
    )
```

profile of v0, /device:TPU:1, one launch (start us, length us, event | category | flops | bytes accessed | tf_op | source)
XLA Modules:
  0.0 237.3 jit_solution(16345921929849043165)
XLA Ops:
  7.2 0.0 copy-start
  7.2 0.0 copy-start.1
  7.2 0.0 all-reduce.2.cloned.1.call-start
  7.2 1.3 copy-done
  8.6 2.4 %convolution_convert_fusion = bf16[256,1024]{1,0:T(8,128)(2,1)} fusion(bf16[256,768]{1,0:T(8,128)(2,1)} %param.6, bf16[1024,768]{1,0:T(8,128)(2,1)S(1)} %copy-done), kind=kOutput, calls=%fused_computation.8 | convolution fusion | flops 402915328 | bytes 2490368 | tf_op jit(solution)/shard_map/dot_general | solution.py:19
  11.0 0.0 copy-start.3
  11.0 0.0 all-reduce.2.cloned.1.call-update
  11.0 0.0 reduce-scatter.8.cloned.1.call-start
  11.0 86.5 %all-reduce.2.cloned.1.call-done = bf16[256,1024]{1,0:T(8,128)(2,1)} async-done(((bf16[256,1024]{1,0:T(8,128)(2,1)}), bf16[256,1024]{1,0:T(8,128)(2,1)}) %all-reduce.2.cloned.1.call-update) | async-done | bytes 524304 | tf_op jit(solution)/shard_map/psum | solution.py:22
  97.6 0.0 copy-done.1
  97.6 1.5 fusion.8
  99.1 0.0 copy-done.3
  99.1 1.8 fusion
  100.9 0.0 reduce-scatter.8.cloned.1.call-update
  100.9 0.0 copy-start.2
  101.0 0.0 reduce-scatter.6.cloned.1.call-start
  101.0 2.8 %convolution_convert_fusion.1 = bf16[256,768]{0,1:T(8,128)(2,1)} fusion(bf16[256,1024]{1,0:T(8,128)(2,1)S(1)} %fusion.8, bf16[768,1024]{1,0:T(8,128)(2,1)} %param.8), kind=kOutput, calls=%fused_computation.9 | convolution fusion | flops 402849792 | bytes 2490368 | tf_op jit(solution)/shard_map/dot_general | solution.py:24
  103.8 0.0 reduce-scatter.6.cloned.1.call-update
  103.8 0.0 reduce-scatter.10.cloned.1.call-start
  103.9 0.0 copy-done.2
  103.9 1.8 multiply_convert_fusion
  105.7 1.6 copy.15
  107.4 0.0 reduce-scatter.10.cloned.1.call-update
  107.4 36.4 %reduce-scatter.8.cloned.1.call-done = bf16[768,128]{0,1:T(8,128)(2,1)} async-done(((bf16[768,1024]{0,1:T(8,128)(2,1)}), bf16[768,128]{0,1:T(8,128)(2,1)}) %reduce-scatter.8.cloned.1.call-update) | async-done | bytes 196624 | tf_op jit(solution)/shard_map/reduce_scatter | solution.py:44
  143.8 1.7 copy.12
  145.5 43.6 %reduce-scatter.6.cloned.1.call-done = bf16[256,96]{0,1:T(8,128)(2,1)} async-done(((bf16[256,768]{0,1:T(8,128)(2,1)}), bf16[256,96]{0,1:T(8,128)(2,1)}) %reduce-scatter.6.cloned.1.call-update) | async-done | bytes 49168 | tf_op jit(solution)/shard_map/reduce_scatter | solution.py:27
  189.1 41.7 %reduce-scatter.10.cloned.1.call-done = bf16[96,1024]{1,0:T(8,128)(2,1)} async-done(((bf16[768,1024]{1,0:T(8,128)(2,1)}), bf16[96,1024]{1,0:T(8,128)(2,1)}) %reduce-scatter.10.cloned.1.call-update) | async-done | bytes 196624
Async XLA Ops:
  7.2 1.4 copy-start
  7.2 90.4 %copy-start.1 = (bf16[256,1024]{1,0:T(8,128)(2,1)S(1)}, bf16[256,1024]{1,0:T(8,128)(2,1)}, u32[]{:S(2)}) copy-start(bf16[256,1024]{1,0:T(8,128)(2,1)} %param.7) | copy-start | bytes 1572868
  7.2 90.4 %all-reduce.2.cloned.1.call-start = ((), (), s32[]{:S(2)}) async-start(), calls=%async_computation.3 | async-start | bytes 1048576 | tf_op jit(solution)/shard_map/psum | solution.py:22
  11.0 88.1 %copy-start.3 = (bf16[256,768]{1,0:T(8,128)(2,1)S(1)}, bf16[256,768]{1,0:T(8,128)(2,1)}, u32[]{:S(2)}) copy-start(bf16[256,768]{1,0:T(8,128)(2,1)} %param.5) | copy-start | bytes 1179652
  11.0 132.8 %reduce-scatter.8.cloned.1.call-start = ((), (), s32[]{:S(2)}) async-start(), calls=%async_computation.5 | async-start | bytes 1769472 | tf_op jit(solution)/shard_map/reduce_scatter | solution.py:44
  100.9 2.9 %copy-start.2 = (bf16[256,768]{1,0:T(8,128)(2,1)S(1)}, bf16[256,768]{1,0:T(8,128)(2,1)}, u32[]{:S(2)}) copy-start(bf16[256,768]{1,0:T(8,128)(2,1)} %param.6) | copy-start | bytes 1179652
  101.0 88.1 %reduce-scatter.6.cloned.1.call-start = ((), (), s32[]{:S(2)}) async-start(), calls=%async_computation.4 | async-start | bytes 442368 | tf_op jit(solution)/shard_map/reduce_scatter | solution.py:27
  103.8 126.9 %reduce-scatter.10.cloned.1.call-start = ((), (), s32[]{:S(2)}) async-start(), calls=%async_computation.6 | async-start | bytes 1769472
Sparse Core Ops, SparseCore 0:
  11.1 86.4 all-reduce.1
  101.1 42.6 reduce-scatter.7
  147.4 41.6 reduce-scatter.5
  192.4 38.3 reduce-scatter.9
where the time goes:
time: 241 us; the launch traced here: 237 us
  waiting for transfers between devices  208 us (86%)
  between operations  13.8 us (6%)
  matrix products  8.81 us (4%)
  local copies, waits for them, and re-layouts  4.74 us (2%)
    psum x1, waiting for transfers between devices, per_device(): lax.psum(partial_act.astype(jnp.bfloat16), 'in').astype(jnp.float32)  86.5 us
    reduce_scatter x1, waiting for transfers between devices, per_device(): lax.psum_scatter(input_term.astype(jnp.bfloat16), 'out', scatter_dimensio...  43.6 us
    unnamed x5, waiting for transfers between devices  41.8 us
    reduce_scatter x1, waiting for transfers between devices, per_device(): lax.psum_scatter(w_in_term.astype(jnp.bfloat16), 'batch', scatter_dimensi...  36.4 us
  transfers between devices with their start and end apart: 4, of which 4 were waited for; matrix products, arithmetic and copies ran while one was open for 3% of the time, Pallas kernels for 0%

commit v1 on v0

v1 whole, which is shorter than its diff:
```python
import math

import jax
import jax.numpy as jnp
from jax import lax
from jax.sharding import Mesh, PartitionSpec as P

BF = jnp.bfloat16
F32 = jnp.float32
IN = ("x", "zlo")
OUT = ("zhi", "core")
SWAP = [(0, 1), (1, 0)]


def cdf_of(value):
    return 0.5 * (1.0 + lax.erf(value * 0.7071067811865476))


def density_of(value):
    return jnp.exp(-0.5 * value * value) * 0.3989422804014327


def nt(a, b):
    return lax.dot_general(a, b, (((1,), (1,)), ((), ())), preferred_element_type=F32)


def tn(a, b):
    return lax.dot_general(a, b, (((0,), (0,)), ((), ())), preferred_element_type=F32)


def per_device(inputs, out_grad, pre_act, w_in, w_out):
    tok, d_in = inputs.shape
    hid = pre_act.shape[1]
    n_in, n_b = 8, 8
    core = lax.axis_index("core")
    y = lax.axis_index("batch")
    i = lax.axis_index(IN)
    factor = 1.0 / math.sqrt(tok * n_b)
    rows = tok // n_in
    ring = [(b, (b + 1) % n_b) for b in range(n_b)] + [
        (n_b + b, n_b + (b - 1) % n_b) for b in range(n_b)
    ]

    part = nt(out_grad, w_out).astype(BF).reshape(n_in, rows, hid)
    got = lax.all_to_all(part, IN, 0, 0, tiled=True)
    act_grad = jnp.sum(got.astype(F32), axis=0)
    v = lax.dynamic_slice_in_dim(pre_act, i * rows, rows, 0).astype(F32)
    deriv = cdf_of(v) + v * density_of(v)
    mine = (act_grad * deriv).astype(BF)
    pre_grad = lax.all_to_all(
        jnp.broadcast_to(mine, (n_in, rows, hid)), IN, 0, 0, tiled=True
    ).reshape(tok, hid)

    x1 = lax.ppermute(inputs, ("core", "batch"), ring)
    x2 = lax.ppermute(x1, ("core", "batch"), ring)
    x3 = lax.ppermute(x2, ("core", "batch"), ring)
    half = lax.dynamic_slice_in_dim(x3, core * (tok // 2), tok // 2, 0)
    x4 = lax.ppermute(half, ("core", "batch"), ring)
    side = jnp.concatenate([x1, x2, x3, x4], 0)
    other = lax.ppermute(side, "core", SWAP)

    pa = pre_act.astype(F32)
    act = (pa * cdf_of(pa)).astype(BF)
    w_out_term = (tn(out_grad, act) * factor).astype(BF)
    w_out_grad = lax.psum_scatter(w_out_term, "batch", scatter_dimension=0, tiled=True).T

    w4 = w_in.reshape(4, 2, d_in // 8, hid)
    w_far = lax.dynamic_index_in_dim(w4, 1 - core, 1, False).reshape(d_in // 2, hid)
    w_near = lax.dynamic_index_in_dim(w4, core, 1, False).reshape(d_in // 2, hid)
    far = nt(w_far, pre_grad).astype(BF)
    near = nt(w_near, pre_grad)
    pair = (near + lax.ppermute(far, "core", SWAP).astype(F32)).astype(BF)
    quad = lax.all_to_all(pair.reshape(4, d_in // 8, tok), "zhi", 0, 0, tiled=True)
    input_grad = jnp.sum(quad.astype(F32), axis=0).astype(BF).T

    cols = pre_grad.reshape(tok, n_b, hid // n_b).swapaxes(0, 1)
    pg = lax.all_to_all(cols, "batch", 0, 0, tiled=True)
    sign = 1 - 2 * core
    take = lambda k: lax.dynamic_index_in_dim(pg, (y + k + n_b) % n_b, 0, False)
    opp = take(4)
    opp_a = lax.dynamic_slice_in_dim(opp, core * (tok // 2), tok // 2, 0)
    opp_b = lax.dynamic_slice_in_dim(opp, (1 - core) * (tok // 2), tok // 2, 0)
    left = jnp.concatenate([inputs, side, other], 0)
    right = jnp.concatenate(
        [pg[y], take(-sign), take(-2 * sign), take(-3 * sign), opp_a]
        + [take(sign), take(2 * sign), take(3 * sign), opp_b],
        0,
    )
    w_in_grad = (tn(left, right) * factor).astype(BF)
    return (input_grad, w_in_grad, w_out_grad)


def solution(mesh):
    fine = Mesh(mesh.devices.reshape(4, 2, 4, 2, 8), ("x", "zlo", "zhi", "core", "batch"))
    return jax.shard_map(
        per_device,
        mesh=fine,
        in_specs=(
            P("batch", IN),
            P("batch", IN),
            P("batch", OUT),
            P(IN, OUT),
            P(OUT, IN),
        ),
        out_specs=(P("batch", IN + OUT), P(IN, OUT + ("batch",)), P(OUT, IN + ("batch",))),
        check_vma=False,
    )
```

time: 241 us -> 132 us (0.55); the launches traced: 237 us -> 131 us
  waiting for transfers between devices: 208 us -> 34.3 us
  starting transfers between devices: 0.16 us -> 50.5 us
  local copies, waits for them, and re-layouts: 4.74 us -> 16.8 us
  matrix products: 8.81 us -> 11.3 us
    psum x1 -> x0, waiting for transfers between devices: 86.5 us -> none  [per_device(): lax.psum(partial_act.astype(jnp.bfloat16), 'in').astype(jnp.float32)]
    reduce_scatter x2 -> x0, waiting for transfers between devices: 80 us -> none  [the longest x1 43.6 us: per_device(): lax.psum_scatter(input_term.astype(jnp.bfloat16), 'out', scatter_dimensio...]
    unnamed x5 -> x2, waiting for transfers between devices: 41.8 us -> 0.02 us
    ppermute x0 -> x6, starting transfers between devices: none -> 26.5 us  [the longest x1 6.73 us: per_device(): x1 = lax.ppermute(inputs, ('core', 'batch'), ring)]
    all_to_all x0 -> x4, starting transfers between devices: none -> 24 us  [the longest x1 8.2 us: per_device(): lax.all_to_all(pair.reshape(4, d_in // 8, tok), 'zhi', 0, 0, tiled=True)]
    ppermute x0 -> x6, waiting for transfers between devices: none -> 18.5 us  [the longest x1 15.9 us: per_device(): x4 = lax.ppermute(half, ('core', 'batch'), ring)]
    all_to_all x0 -> x4, waiting for transfers between devices: none -> 15.8 us  [the longest x1 8.28 us: per_device(): lax.all_to_all(pair.reshape(4, d_in // 8, tok), 'zhi', 0, 0, tiled=True)]
    unnamed x10 -> x23, local copies, waits for them, and re-layouts: 4.74 us -> 10.1 us
  transfers between devices with their start and end apart: 4 -> 11, of which waited for: 4 -> 4; matrix products, arithmetic and copies ran while one was open for 3% -> 20% of each run, Pallas kernels for 0% -> 0%
where the time goes in v1:
time: 132 us; the launch traced here: 131 us
  starting transfers between devices  50.5 us (38%)
  waiting for transfers between devices  34.3 us (26%)
  local copies, waits for them, and re-layouts  16.8 us (13%)
  between operations  14.2 us (11%)
  matrix products  11.3 us (9%)
  other arithmetic  3.83 us (3%)
    ppermute x1, waiting for transfers between devices, per_device(): x4 = lax.ppermute(half, ('core', 'batch'), ring)  15.9 us
    unnamed x23, local copies, waits for them, and re-layouts  10.1 us
    all_to_all x1, waiting for transfers between devices, per_device(): lax.all_to_all(pair.reshape(4, d_in // 8, tok), 'zhi', 0, 0, tiled=True)  8.28 us
    all_to_all x1, starting transfers between devices, per_device(): lax.all_to_all(pair.reshape(4, d_in // 8, tok), 'zhi', 0, 0, tiled=True)  8.2 us
    all_to_all x1, waiting for transfers between devices, per_device(): got = lax.all_to_all(part, IN, 0, 0, tiled=True)  7.54 us
    ppermute x1, starting transfers between devices, per_device(): x1 = lax.ppermute(inputs, ('core', 'batch'), ring)  6.73 us
    dot_general x2, matrix products, tn(): lax.dot_general(a, b, (((0,), (0,)), ((), ())), preferred_element_type=F32)  6.68 us
    all_to_all x1, starting transfers between devices, per_device(): got = lax.all_to_all(part, IN, 0, 0, tiled=True)  6.66 us
  transfers between devices with their start and end apart: 11, of which 4 were waited for; matrix products, arithmetic and copies ran while one was open for 20% of the time, Pallas kernels for 0%

profile of v1, /device:TPU:1, one launch (start us, length us, event | category | flops | bytes accessed | tf_op | source)
XLA Modules:
  0.0 130.9 jit_solution(3256706277750314909)
XLA Ops:
  7.2 1.4 %copy-done = bf16[1024,768]{1,0:T(8,128)(2,1)S(1)} copy-done((bf16[1024,768]{1,0:T(8,128)(2,1)S(1)}, bf16[1024,768]{1,0:T(8,128)(2,1)}, u32[]{:S(2)}) %copy-start) | copy-done | bytes 1572888
  8.6 2.4 %convolution_convert_fusion = bf16[256,1024]{1,0:T(8,128)(2,1)} fusion(bf16[256,768]{1,0:T(8,128)(2,1)} %param.6, bf16[1024,768]{1,0:T(8,128)(2,1)S(1)} %copy-done), kind=kOutput, calls=%fused_computation.5 | convolution fusion | flops 402915328 | bytes 2490368 | tf_op jit(solution)/shard_map/dot_general | solution.py:24
  11.0 6.7 %all-to-all-start = ((bf16[8,32,1024]{2,1,0:T(8,128)(2,1)}), bf16[8,32,1024]{2,1,0:T(8,128)(2,1)S(1)}, u32[]{:S(2)}, u32[]{:S(2)}) async-start(bf16[8,32,1024]{2,1,0:T(8,128)(2,1)} %bitcast.2), calls=%async_computation | async-start | bytes 1048576 | tf_op jit(solution)/shard_map/all_to_all | solution.py:45
  17.6 7.5 %all-to-all-done = bf16[8,32,1024]{2,1,0:T(8,128)(2,1)S(1)} async-done(((bf16[8,32,1024]{2,1,0:T(8,128)(2,1)}), bf16[8,32,1024]{2,1,0:T(8,128)(2,1)S(1)}, u32[]{:S(2)}, u32[]{:S(2)}) %all-to-all-start) | async-done | bytes 524320 | tf_op jit(solution)/shard_map/all_to_all | solution.py:45
  25.3 0.9 fusion.17
  26.2 0.9 broadcast_in_dim.3
  27.0 3.5 %all-to-all-start.1 = ((bf16[8,32,1024]{2,1,0:T(8,128)(2,1)}), bf16[8,32,1024]{2,1,0:T(8,128)(2,1)S(1)}, u32[]{:S(2)}, u32[]{:S(2)}) async-start(bf16[8,32,1024]{2,1,0:T(8,128)(2,1)} %broadcast_in_dim.3), calls=%async_computation.1 | async-start | bytes 1048576 | tf_op jit(solution)/shard_map/all_to_all | solution.py:50
  30.6 6.7 %collective-permute-start.1 = (bf16[256,768]{1,0:T(8,128)(2,1)}, bf16[256,768]{1,0:T(8,128)(2,1)S(1)}, u32[]{:S(2)}, u32[]{:S(2)}) collective-permute-start(bf16[256,768]{1,0:T(8,128)(2,1)} %param.5), channel_id=1, source_target_pairs={{0,1},{1,2},{2,3},{3,4},{4,5},{5,6},{6,7},{7,0},{8,15},{9,8},{10,9... | collective-permute-start | bytes 1179656 | tf_op jit(solution)/shard_map/ppermute | solution.py:54
  37.3 2.4 %constant_dynamic-slice_fusion.1 = (bf16[4,1,96,1024]{3,2,1,0:T(8,128)(2,1)S(1)}, bf16[4,1,96,1024]{3,2,1,0:T(8,128)(2,1)}) fusion(bf16[4,2,96,1024]{3,2,1,0:T(8,128)(2,1)} %bitcast.50, s32[]{:T(128)S(6)} %select_n.81, s32[]{:T(128)S(6)} %select_n.79), kind=kLoop, calls=%fused_computation.46 | loop fusion | bytes 3145736 | tf_op jit(solution)/shard_map/jit(dynamic_index_in_dim)/dynamic_slice | solution.py:68
  39.7 2.6 %collective-permute-done.1 = bf16[256,768]{1,0:T(8,128)(2,1)S(1)} collective-permute-done((bf16[256,768]{1,0:T(8,128)(2,1)}, bf16[256,768]{1,0:T(8,128)(2,1)S(1)}, u32[]{:S(2)}, u32[]{:S(2)}) %collective-permute-start.1) | collective-permute-done | bytes 393248 | tf_op jit(solution)/shard_map/ppermute | solution.py:54
  42.3 5.2 %collective-permute-start.2 = (bf16[256,768]{1,0:T(8,128)(2,1)S(1)}, bf16[256,768]{1,0:T(8,128)(2,1)}, u32[]{:S(2)}, u32[]{:S(2)}) collective-permute-start(bf16[256,768]{1,0:T(8,128)(2,1)S(1)} %collective-permute-done.1), channel_id=1, source_target_pairs={{0,1},{1,2},{2,3},{3,4},{4,5},{5,6},{6,7},{7,0},{8,15},{9,8},{10,9... | collective-permute-start | bytes 1179656 | tf_op jit(solution)/shard_map/ppermute | solution.py:55
  47.6 1.1 convolution_convert_fusion.1
  48.6 2.7 %collective-permute-start = (bf16[384,256]{1,0:T(8,128)(2,1)}, bf16[384,256]{1,0:T(8,128)(2,1)S(1)}, u32[]{:S(2)}, u32[]{:S(2)}) collective-permute-start(bf16[384,256]{1,0:T(8,128)(2,1)} %convolution_convert_fusion.1), channel_id=1, source_target_pairs={{0,8},{8,0},{1,9},{9,1},{2,10},{10,2},{3,11},{11,3},{4,12},{12,4},... | collective-permute-start | bytes 589832 | tf_op jit(solution)/shard_map/ppermute | solution.py:72
  51.4 3.1 %fusion = bf16[768,1024]{0,1:T(8,128)(2,1)} fusion(bf16[256,768]{1,0:T(8,128)(2,1)} %param.6, bf16[256,1024]{1,0:T(8,128)(2,1)} %param.7), kind=kOutput, calls=%fused_computation.1 | convolution fusion | flops 405798912 | bytes 2490368 | tf_op jit(solution)/shard_map/dot_general | solution.py:28
  54.5 2.6 %copy.13 = bf16[768,1024]{1,0:T(8,128)(2,1)} copy(bf16[768,1024]{0,1:T(8,128)(2,1)} %fusion) | data formatting | bytes 3145728
  57.2 4.9 %collective-permute-start.3 = (bf16[256,768]{1,0:T(8,128)(2,1)}, bf16[256,768]{1,0:T(8,128)(2,1)S(1)}, u32[]{:S(2)}, u32[]{:S(2)}) collective-permute-start(bf16[256,768]{1,0:T(8,128)(2,1)} %collective-permute-done.2), channel_id=1, source_target_pairs={{0,1},{1,2},{2,3},{3,4},{4,5},{5,6},{6,7},{7,0},{8,15},{9,8},{10,9... | collective-permute-start | bytes 1179656 | tf_op jit(solution)/shard_map/ppermute | solution.py:56
  62.0 1.1 add_convert_fusion
  63.1 8.2 %all-to-all-start.2 = ((bf16[4,96,256]{2,1,0:T(8,128)(2,1)}), bf16[4,96,256]{2,1,0:T(8,128)(2,1)S(1)}, u32[]{:S(2)}, u32[]{:S(2)}) async-start(bf16[4,96,256]{2,1,0:T(8,128)(2,1)} %bitcast.5), calls=%async_computation.2 | async-start | bytes 393216 | tf_op jit(solution)/shard_map/all_to_all | solution.py:73
  71.4 0.9 copy.11
  72.3 8.3 %all-to-all-done.2 = bf16[4,96,256]{2,1,0:T(8,128)(2,1)S(1)} async-done(((bf16[4,96,256]{2,1,0:T(8,128)(2,1)}), bf16[4,96,256]{2,1,0:T(8,128)(2,1)S(1)}, u32[]{:S(2)}, u32[]{:S(2)}) %all-to-all-start.2) | async-done | bytes 196640 | tf_op jit(solution)/shard_map/all_to_all | solution.py:73
  80.6 5.6 %all-to-all-start.3 = ((bf16[8,256,128]{2,1,0:T(8,128)(2,1)}), bf16[8,256,128]{2,1,0:T(8,128)(2,1)S(1)}, u32[]{:S(2)}, u32[]{:S(2)}) async-start(bf16[8,256,128]{2,1,0:T(8,128)(2,1)} %copy.11), calls=%async_computation.3 | async-start | bytes 1048576 | tf_op jit(solution)/shard_map/all_to_all | solution.py:77
  86.3 4.6 %collective-permute-start.4 = (bf16[128,768]{1,0:T(8,128)(2,1)S(1)}, bf16[128,768]{1,0:T(8,128)(2,1)S(1)}, u32[]{:S(2)}, u32[]{:S(2)}) collective-permute-start(bf16[128,768]{1,0:T(8,128)(2,1)S(1)} %constant_dynamic-slice_fusion), channel_id=1, source_target_pairs={{0,1},{1,2},{2,3},{3,4},{4,5},{5,6},{6,7},{7,0},{8,15},{9,8},{10,9... | collective-permute-start | bytes 589832 | tf_op jit(solution)/shard_map/ppermute | solution.py:58
  90.9 1.8 %constant_dynamic-update-slice_fusion.5 = bf16[2048,768]{1,0:T(8,128)(2,1)} fusion(bf16[256,768]{1,0:T(8,128)(2,1)} %param.5), kind=kLoop, calls=%fused_computation.42 | loop fusion | bytes 786432
  92.6 0.8 constant_dynamic-update-slice_fusion.4
  93.4 15.9 %collective-permute-done.4 = bf16[128,768]{1,0:T(8,128)(2,1)S(1)} collective-permute-done((bf16[128,768]{1,0:T(8,128)(2,1)S(1)}, bf16[128,768]{1,0:T(8,128)(2,1)S(1)}, u32[]{:S(2)}, u32[]{:S(2)}) %collective-permute-start.4) | collective-permute-done | bytes 196640 | tf_op jit(solution)/shard_map/ppermute | solution.py:58
  109.3 2.2 %pad_maximum_fusion = bf16[896,768]{1,0:T(8,128)(2,1)} fusion(bf16[128,768]{1,0:T(8,128)(2,1)S(1)} %collective-permute-done.4, bf16[256,768]{1,0:T(8,128)(2,1)S(1)} %collective-permute-done.3, bf16[256,768]{1,0:T(8,128)(2,1)} %collective-permute-done.2, bf16[256,768]{1,0:T(8,128)(2,1)S(1)} %copy-done.3), kind=kLoop, calls=%fused_computation.2 | loop fusion | flops 5505024 | bytes 2752512 | tf_op jit(solution)/shard_map/concatenate | solution.py:59
  111.5 2.4 %collective-permute-start.5 = (bf16[896,768]{1,0:T(8,128)(2,1)}, bf16[896,768]{1,0:T(8,128)(2,1)}, u32[]{:S(2)}, u32[]{:S(2)}) collective-permute-start(bf16[896,768]{1,0:T(8,128)(2,1)} %pad_maximum_fusion), channel_id=1, source_target_pairs={{0,8},{8,0},{1,9},{9,1},{2,10},{10,2},{3,11},{11,3},{4,12},{12,4},... | collective-permute-start | bytes 4128776 | tf_op jit(solution)/shard_map/ppermute | solution.py:60
  113.8 1.8 %constant_dynamic-update-slice_fusion.3 = bf16[2048,768]{1,0:T(8,128)(2,1)} fusion(bf16[2048,768]{1,0:T(8,128)(2,1)} %constant_dynamic-update-slice_fusion.4, bf16[256,768]{1,0:T(8,128)(2,1)} %collective-permute-done.2), kind=kLoop, calls=%fused_computation.40 | loop fusion | bytes 786432
  115.6 0.8 constant_dynamic-update-slice_fusion.2
  116.4 0.7 constant_dynamic-update-slice_fusion.1
  118.0 2.5 %constant_dynamic-update-slice_fusion = bf16[2048,768]{1,0:T(8,128)(2,1)} fusion(bf16[2048,768]{1,0:T(8,128)(2,1)} %constant_dynamic-update-slice_fusion.1, bf16[896,768]{1,0:T(8,128)(2,1)} %collective-permute-done.5), kind=kLoop, calls=%fused_computation.37 | loop fusion | bytes 2752512 | tf_op jit(solution)/shard_map/concatenate | solution.py:83
  120.5 3.6 %fusion.1 = bf16[768,128]{1,0:T(8,128)(2,1)} fusion(bf16[2048,768]{1,0:T(8,128)(2,1)} %constant_dynamic-update-slice_fusion, bf16[2048,128]{1,0:T(8,128)(2,1)S(1)} %constant_dynamic-update-slice_fusion.6), kind=kOutput, calls=%fused_computation.7 | convolution fusion | flops 402849792 | bytes 3866624 | tf_op jit(solution)/shard_map/dot_general | solution.py:28
  (29 shorter events, 1.1 us)
Async XLA Ops:
  7.2 1.4 %copy-start = (bf16[1024,768]{1,0:T(8,128)(2,1)S(1)}, bf16[1024,768]{1,0:T(8,128)(2,1)}, u32[]{:S(2)}) copy-start(bf16[1024,768]{1,0:T(8,128)(2,1)} %param.9) | copy-start | bytes 4718596
  11.0 14.2 %all-to-all-start = ((bf16[8,32,1024]{2,1,0:T(8,128)(2,1)}), bf16[8,32,1024]{2,1,0:T(8,128)(2,1)S(1)}, u32[]{:S(2)}, u32[]{:S(2)}) async-start(bf16[8,32,1024]{2,1,0:T(8,128)(2,1)} %bitcast.2), calls=%async_computation | async-start | bytes 1048576 | tf_op jit(solution)/shard_map/all_to_all | solution.py:45
  27.0 20.5 %all-to-all-start.1 = ((bf16[8,32,1024]{2,1,0:T(8,128)(2,1)}), bf16[8,32,1024]{2,1,0:T(8,128)(2,1)S(1)}, u32[]{:S(2)}, u32[]{:S(2)}) async-start(bf16[8,32,1024]{2,1,0:T(8,128)(2,1)} %broadcast_in_dim.3), calls=%async_computation.1 | async-start | bytes 1048576 | tf_op jit(solution)/shard_map/all_to_all | solution.py:50
  30.5 93.6 %reduce-scatter.4.cloned.1.call-start = ((), (), s32[]{:S(2)}) async-start(), calls=%async_computation.5 | async-start | bytes 1769472
  30.6 11.8 %collective-permute-start.1 = (bf16[256,768]{1,0:T(8,128)(2,1)}, bf16[256,768]{1,0:T(8,128)(2,1)S(1)}, u32[]{:S(2)}, u32[]{:S(2)}) collective-permute-start(bf16[256,768]{1,0:T(8,128)(2,1)} %param.5), channel_id=1, source_target_pairs={{0,1},{1,2},{2,3},{3,4},{4,5},{5,6},{6,7},{7,0},{8,15},{9,8},{10,9... | collective-permute-start | bytes 1179656 | tf_op jit(solution)/shard_map/ppermute | solution.py:54
  42.3 14.8 %copy-start.2 = (bf16[256,768]{1,0:T(8,128)(2,1)}, bf16[256,768]{1,0:T(8,128)(2,1)S(1)}, u32[]{:S(2)}) copy-start(bf16[256,768]{1,0:T(8,128)(2,1)S(1)} %collective-permute-done.1) | copy-start | bytes 1179652
  42.3 14.8 %collective-permute-start.2 = (bf16[256,768]{1,0:T(8,128)(2,1)S(1)}, bf16[256,768]{1,0:T(8,128)(2,1)}, u32[]{:S(2)}, u32[]{:S(2)}) collective-permute-start(bf16[256,768]{1,0:T(8,128)(2,1)S(1)} %collective-permute-done.1), channel_id=1, source_target_pairs={{0,1},{1,2},{2,3},{3,4},{4,5},{5,6},{6,7},{7,0},{8,15},{9,8},{10,9... | collective-permute-start | bytes 1179656 | tf_op jit(solution)/shard_map/ppermute | solution.py:55
  48.6 13.4 %collective-permute-start = (bf16[384,256]{1,0:T(8,128)(2,1)}, bf16[384,256]{1,0:T(8,128)(2,1)S(1)}, u32[]{:S(2)}, u32[]{:S(2)}) collective-permute-start(bf16[384,256]{1,0:T(8,128)(2,1)} %convolution_convert_fusion.1), channel_id=1, source_target_pairs={{0,8},{8,0},{1,9},{9,1},{2,10},{10,2},{3,11},{11,3},{4,12},{12,4},... | collective-permute-start | bytes 589832 | tf_op jit(solution)/shard_map/ppermute | solution.py:72
  54.5 7.6 %copy-start.1 = (bf16[4,1,96,1024]{3,2,1,0:T(8,128)(2,1)S(1)}, bf16[4,1,96,1024]{3,2,1,0:T(8,128)(2,1)}, u32[]{:S(2)}) copy-start(bf16[4,1,96,1024]{3,2,1,0:T(8,128)(2,1)} %get-tuple-element.16) | copy-start | bytes 2359300
  57.2 29.1 %collective-permute-start.3 = (bf16[256,768]{1,0:T(8,128)(2,1)}, bf16[256,768]{1,0:T(8,128)(2,1)S(1)}, u32[]{:S(2)}, u32[]{:S(2)}) collective-permute-start(bf16[256,768]{1,0:T(8,128)(2,1)} %collective-permute-done.2), channel_id=1, source_target_pairs={{0,1},{1,2},{2,3},{3,4},{4,5},{5,6},{6,7},{7,0},{8,15},{9,8},{10,9... | collective-permute-start | bytes 1179656 | tf_op jit(solution)/shard_map/ppermute | solution.py:56
  63.1 29.5 %copy-start.3 = (bf16[256,768]{1,0:T(8,128)(2,1)S(1)}, bf16[256,768]{1,0:T(8,128)(2,1)}, u32[]{:S(2)}) copy-start(bf16[256,768]{1,0:T(8,128)(2,1)} %copy-done.2) | copy-start | bytes 1179652
  63.1 17.5 %all-to-all-start.2 = ((bf16[4,96,256]{2,1,0:T(8,128)(2,1)}), bf16[4,96,256]{2,1,0:T(8,128)(2,1)S(1)}, u32[]{:S(2)}, u32[]{:S(2)}) async-start(bf16[4,96,256]{2,1,0:T(8,128)(2,1)} %bitcast.5), calls=%async_computation.2 | async-start | bytes 393216 | tf_op jit(solution)/shard_map/all_to_all | solution.py:73
  80.6 37.1 %all-to-all-start.3 = ((bf16[8,256,128]{2,1,0:T(8,128)(2,1)}), bf16[8,256,128]{2,1,0:T(8,128)(2,1)S(1)}, u32[]{:S(2)}, u32[]{:S(2)}) async-start(bf16[8,256,128]{2,1,0:T(8,128)(2,1)} %copy.11), calls=%async_computation.3 | async-start | bytes 1048576 | tf_op jit(solution)/shard_map/all_to_all | solution.py:77
  86.3 23.0 %collective-permute-start.4 = (bf16[128,768]{1,0:T(8,128)(2,1)S(1)}, bf16[128,768]{1,0:T(8,128)(2,1)S(1)}, u32[]{:S(2)}, u32[]{:S(2)}) collective-permute-start(bf16[128,768]{1,0:T(8,128)(2,1)S(1)} %constant_dynamic-slice_fusion), channel_id=1, source_target_pairs={{0,1},{1,2},{2,3},{3,4},{4,5},{5,6},{6,7},{7,0},{8,15},{9,8},{10,9... | collective-permute-start | bytes 589832 | tf_op jit(solution)/shard_map/ppermute | solution.py:58
  111.5 6.5 %collective-permute-start.5 = (bf16[896,768]{1,0:T(8,128)(2,1)}, bf16[896,768]{1,0:T(8,128)(2,1)}, u32[]{:S(2)}, u32[]{:S(2)}) collective-permute-start(bf16[896,768]{1,0:T(8,128)(2,1)} %pad_maximum_fusion), channel_id=1, source_target_pairs={{0,8},{8,0},{1,9},{9,1},{2,10},{10,2},{3,11},{11,3},{4,12},{12,4},... | collective-permute-start | bytes 4128776 | tf_op jit(solution)/shard_map/ppermute | solution.py:60
Sparse Core Ops, SparseCore 0:
  57.3 50.3 reduce-scatter.3

commit v2 on v0

v2 whole, which is shorter than its diff:
```python
import functools
import math

import jax
import jax.numpy as jnp
from jax import lax
from jax.experimental import pallas as pl
from jax.experimental.pallas import tpu as pltpu
from jax.sharding import Mesh, PartitionSpec as P

BF = jnp.bfloat16
F32 = jnp.float32
IN = ("x", "zlo")
OUT = ("zhi", "core")
SWAP = [(0, 1), (1, 0)]
N = 8
RING = [(b, (b + 1) % N) for b in range(N)] + [(N + b, N + (b - 1) % N) for b in range(N)]


def sds(shape, dtype=BF):
    return jax.ShapeDtypeStruct(shape, dtype)


def call(body, outs, *args, any_tail=0, flops=0, touched=0):
    vm = pl.BlockSpec(memory_space=pltpu.VMEM)
    hold = pl.BlockSpec(memory_space=pl.ANY)
    many = isinstance(outs, (list, tuple))
    return pl.pallas_call(
        body,
        out_shape=outs,
        in_specs=[vm] * (len(args) - any_tail) + [hold] * any_tail,
        out_specs=[vm] * len(outs) if many else vm,
        compiler_params=pltpu.CompilerParams(vmem_limit_bytes=40 * 1024 * 1024),
    )(*args)


def cdf_of(value):
    return 0.5 * (1.0 + lax.erf(value * 0.7071067811865476))


def density_of(value):
    return jnp.exp(-0.5 * value * value) * 0.3989422804014327


def dot(a, b):
    return jnp.dot(a, b, preferred_element_type=F32)


def ring_sign():
    return 1 - 2 * lax.axis_index("core")


def own_terms(factor, out_grad, pre, terms, turned, deriv):
    y, s = lax.axis_index("batch"), ring_sign()
    v = pre[...].astype(F32)
    act = (v * cdf_of(v)).astype(BF)
    flipped = out_grad[...].T
    turned[...] = flipped
    width = flipped.shape[0] // N
    for k in range(5):
        at = pl.multiple_of(((y + s * k + N) % N) * width, width)
        terms[k] = (dot(turned[pl.ds(at, width), :], act) * factor).astype(BF)
    i = lax.axis_index(IN)
    wide = pre.shape[1] // N
    u = pre[:, pl.ds(pl.multiple_of(i * wide, wide), wide)].astype(F32)
    deriv[...] = (cdf_of(u) + u * density_of(u)).T


def far_terms(factor, turned, pre, terms):
    y, s = lax.axis_index("batch"), ring_sign()
    v = pre[...].astype(F32)
    act = (v * cdf_of(v)).astype(BF)
    width = turned.shape[0] // N
    for k in range(1, 4):
        at = pl.multiple_of(((y + s * k + N) % N) * width, width)
        terms[k - 1] = (dot(turned[pl.ds(at, width), :], act) * factor).astype(BF)


def hidden_grad(got, deriv, out):
    total = got[0].astype(F32)
    for k in range(1, N):
        total = total + got[k].astype(F32)
    mine = (total * deriv[...]).astype(BF)
    for k in range(N):
        out[k] = mine


def first_add(got, own, far, out):
    out[0] = (got[...].astype(F32) + own[3].astype(F32)).astype(BF)
    out[1] = far[2]


def next_add(k, got, own, far, out):
    out[0] = (got[0].astype(F32) + own[k].astype(F32)).astype(BF)
    out[1] = (got[1].astype(F32) + far[k - 1].astype(F32)).astype(BF)


def last_add(got, other, own, out):
    out[...] = (got[0].astype(F32) + other[...].astype(F32) + own[0].astype(F32)).astype(BF)


def send_half(w, pg, out):
    c = lax.axis_index("core")
    width = w.shape[0] // N
    for z in range(4):
        at = pl.multiple_of((2 * z + 1 - c) * width, width)
        out[z] = dot(w[pl.ds(at, width), :], pg[...]).astype(BF)


def keep_half(w, pg, got, *outs):
    c, zhi = lax.axis_index("core"), lax.axis_index("zhi")
    width = w.shape[0] // N
    for s in range(4):
        z = (zhi + s) % 4
        at = pl.multiple_of((2 * z + c) * width, width)
        outs[s][...] = (dot(w[pl.ds(at, width), :], pg[...]) + got[z].astype(F32)).astype(BF)


def sum_four(a, b, c, d, out):
    total = a[...].astype(F32) + b[...].astype(F32) + c[...].astype(F32) + d[...].astype(F32)
    out[...] = total.astype(BF)


def weight_grad(factor, pg, x0, x1, x2, x3, x4, z1, z2, z3, out):
    y, s = lax.axis_index("batch"), ring_sign()
    total = dot(pg[y], x0[...])
    for k, ref in ((-1, x1), (-2, x2), (-3, x3), (4, x4), (1, z1), (2, z2), (3, z3)):
        total = total + dot(pg[(y + s * k + N) % N], ref[...])
    out[...] = (total * factor).T.astype(BF)


def per_device(inputs, out_grad, pre_act, w_in, w_out):
    tok, d_in = inputs.shape
    hid = pre_act.shape[1]
    factor = 1.0 / math.sqrt(tok * N)
    piece, wide = d_in // N, hid // N
    up = lambda a: lax.ppermute(a, ("core", "batch"), RING)
    swap = lambda a: lax.ppermute(a, "core", SWAP)

    x1 = up(inputs)
    pre_far = swap(pre_act)

    part = lax.dot_general(w_out, out_grad, (((1,), (1,)), ((), ())), preferred_element_type=F32)
    got = lax.all_to_all(part.astype(BF).reshape(N, wide, tok), IN, 0, 0, tiled=True)

    own, turned, deriv = call(
        functools.partial(own_terms, factor),
        [sds((5, piece, hid)), sds((d_in, tok)), sds((wide, tok), F32)],
        out_grad,
        pre_act,
    )
    far = call(functools.partial(far_terms, factor), sds((3, piece, hid)), turned, pre_far)
    x2 = up(x1)

    spread = call(hidden_grad, sds((N, wide, tok)), got, deriv)
    pg = lax.all_to_all(spread, IN, 0, 0, tiled=True)

    r1 = up(own[4])
    t2 = call(first_add, sds((2, piece, hid)), r1, own, far)
    x3 = up(x2)

    cols = lax.all_to_all(pg, "batch", 0, 0, tiled=True)
    pg_flat = pg.reshape(hid, tok)
    far_half = call(send_half, sds((4, piece, tok)), w_in, pg_flat)
    kept = call(keep_half, [sds((piece, tok))] * 4, w_in, pg_flat, swap(far_half))
    parts = [kept[0]] + [
        lax.ppermute(kept[s], "zhi", [(z, (z + s) % 4) for z in range(4)]) for s in range(1, 4)
    ]
    input_grad = call(sum_four, sds((piece, tok)), *parts).T

    r2 = up(t2)
    t3 = call(functools.partial(next_add, 2), sds((2, piece, hid)), r2, own, far)
    x4 = up(x3)
    r3 = up(t3)
    t4 = call(functools.partial(next_add, 1), sds((2, piece, hid)), r3, own, far)
    r4 = up(t4)
    w_out_grad = call(last_add, sds((piece, hid)), r4, swap(r4[1]), own).T

    w_in_grad = call(
        functools.partial(weight_grad, factor),
        sds((d_in, wide)),
        cols, inputs, x1, x2, x3, x4, swap(x1), swap(x2), swap(x3),
    )
    return (input_grad, w_in_grad, w_out_grad)


def solution(mesh):
    fine = Mesh(mesh.devices.reshape(4, 2, 4, 2, 8), ("x", "zlo", "zhi", "core", "batch"))
    return jax.shard_map(
        per_device,
        mesh=fine,
        in_specs=(P("batch", IN), P("batch", IN), P("batch", OUT), P(IN, OUT), P(OUT, IN)),
        out_specs=(P("batch", IN + OUT), P(IN, OUT + ("batch",)), P(OUT, IN + ("batch",))),
        check_vma=False,
    )
```

time: 241 us -> 129 us (0.54)
  the two profiles are of different devices: /device:TPU:1 before, /device:TPU:2 now
where the time goes in v2:
time: 129 us; the launch traced here: 128 us
  starting transfers between devices  71.6 us (56%)
  waiting for transfers between devices  25.7 us (20%)
  local copies, waits for them, and re-layouts  14.2 us (11%)
  Pallas kernels  13.1 us (10%)
  matrix products  2.4 us (2%)
    ppermute x8, starting transfers between devices, per_device(): up = lambda a: lax.ppermute(a, ('core', 'batch'), RING)  20.2 us
    ppermute x3, starting transfers between devices, per_device(): lax.ppermute(kept[s], 'zhi', [(z, (z + s) % 4) for z in range(4)])  16.2 us
    ppermute x6, starting transfers between devices, per_device(): swap = lambda a: lax.ppermute(a, 'core', SWAP)  13.8 us
    unnamed x36, local copies, waits for them, and re-layouts  13.5 us
    pallas_call x11, Pallas kernels, call(): pl.pallas_call(body, out_shape=outs, in_specs=[vm] * (len(args) - any_tai...  13.1 us
    ppermute x3, waiting for transfers between devices, per_device(): lax.ppermute(kept[s], 'zhi', [(z, (z + s) % 4) for z in range(4)])  13 us
    ppermute x8, waiting for transfers between devices, per_device(): up = lambda a: lax.ppermute(a, ('core', 'batch'), RING)  11.7 us
    all_to_all x1, starting transfers between devices, per_device(): lax.all_to_all(part.astype(BF).reshape(N, wide, tok), IN, 0, 0, tiled=True)  9.31 us
  transfers between devices with their start and end apart: 20, of which 8 were waited for; matrix products, arithmetic and copies ran while one was open for 1% of the time, Pallas kernels for 8%

profile of v2, /device:TPU:2, one launch (start us, length us, event | category | flops | bytes accessed | tf_op | source)
XLA Modules:
  0.0 127.9 jit_solution(3502198712601450061)
XLA Ops:
  2.0 2.4 %convolution_convert_fusion = bf16[1024,256]{1,0:T(8,128)(2,1)} fusion(bf16[1024,768]{1,0:T(8,128)(2,1)S(1)} %copy-done, bf16[256,768]{1,0:T(8,128)(2,1)} %out_grad.1), kind=kOutput, calls=%fused_computation | convolution fusion | flops 402915328 | bytes 2490368 | tf_op jit(solution)/shard_map/dot_general | solution.py:143
  4.4 9.3 %all-to-all-start = ((bf16[8,128,256]{2,1,0:T(8,128)(2,1)}), bf16[8,128,256]{2,1,0:T(8,128)(2,1)S(1)}, u32[]{:S(2)}, u32[]{:S(2)}) async-start(bf16[8,128,256]{2,1,0:T(8,128)(2,1)} %bitcast), calls=%async_computation | async-start | bytes 1048576 | tf_op jit(solution)/shard_map/all_to_all | solution.py:144
  13.7 1.9 %collective-permute-start.12 = (bf16[256,1024]{1,0:T(8,128)(2,1)}, bf16[256,1024]{1,0:T(8,128)(2,1)}, u32[]{:S(2)}, u32[]{:S(2)}) collective-permute-start(bf16[256,1024]{1,0:T(8,128)(2,1)} %pre.1), channel_id=1, source_target_pairs={{0,8},{8,0},{1,9},{9,1},{2,10},{10,2},{3,11},{11,3},{4,12},{12,4},... | collective-permute-start | bytes 1572872 | tf_op jit(solution)/shard_map/ppermute | solution.py:138
  15.7 1.8 %shard_map.76 = (bf16[5,96,1024]{2,1,0:T(8,128)(2,1)S(1)}, bf16[768,256]{1,0:T(8,128)(2,1)S(1)}, f32[128,256]{1,0:T(8,128)S(1)}) custom-call(bf16[256,768]{1,0:T(8,128)(2,1)S(1)} %copy-done.2, bf16[256,1024]{1,0:T(8,128)(2,1)} %pre.1), custom_call_target="tpu_custom_call" | custom-call | tf_op jit(solution)/shard_map/pallas_call | solution.py:28
  19.0 1.9 %collective-permute-start.11 = (bf16[96,1024]{1,0:T(8,128)(2,1)}, bf16[96,1024]{1,0:T(8,128)(2,1)}, u32[]{:S(2)}, u32[]{:S(2)}) collective-permute-start(bf16[96,1024]{1,0:T(8,128)(2,1)} %slice_bitcast_fusion.1), channel_id=1, source_target_pairs={{0,1},{1,2},{2,3},{3,4},{4,5},{5,6},{6,7},{7,0},{8,15},{9,8},{10,9... | collective-permute-start | bytes 589832 | tf_op jit(solution)/shard_map/ppermute | solution.py:137
  22.8 5.7 %all-to-all-start.1 = ((bf16[8,128,256]{2,1,0:T(8,128)(2,1)}), bf16[8,128,256]{2,1,0:T(8,128)(2,1)}, u32[]{:S(2)}, u32[]{:S(2)}) async-start(bf16[8,128,256]{2,1,0:T(8,128)(2,1)} %shard_map.77), calls=%async_computation.1 | async-start | bytes 1048576 | tf_op jit(solution)/shard_map/all_to_all | solution.py:156
  28.5 2.4 %collective-permute-start.4 = (bf16[256,768]{1,0:T(8,128)(2,1)}, bf16[256,768]{1,0:T(8,128)(2,1)S(1)}, u32[]{:S(2)}, u32[]{:S(2)}) collective-permute-start(bf16[256,768]{1,0:T(8,128)(2,1)} %x0.1), channel_id=1, source_target_pairs={{0,1},{1,2},{2,3},{3,4},{4,5},{5,6},{6,7},{7,0},{8,15},{9,8},{10,9... | collective-permute-start | bytes 1179656 | tf_op jit(solution)/shard_map/ppermute | solution.py:137
  30.9 1.6 %shard_map.82.far = bf16[3,96,1024]{2,1,0:T(8,128)(2,1)S(1)} custom-call(bf16[768,256]{1,0:T(8,128)(2,1)S(1)} %copy-done.15, bf16[256,1024]{1,0:T(8,128)(2,1)} %collective-permute-done.12.pre), custom_call_target="tpu_custom_call" | custom-call | tf_op jit(solution)/shard_map/pallas_call | solution.py:28
  33.5 3.5 %collective-permute-start.13 = (bf16[2,96,1024]{2,1,0:T(8,128)(2,1)S(1)}, bf16[2,96,1024]{2,1,0:T(8,128)(2,1)S(1)}, u32[]{:S(2)}, u32[]{:S(2)}) collective-permute-start(bf16[2,96,1024]{2,1,0:T(8,128)(2,1)S(1)} %shard_map.83), channel_id=1, source_target_pairs={{0,1},{1,2},{2,3},{3,4},{4,5},{5,6},{6,7},{7,0},{8,15},{9,8},{10,9... | collective-permute-start | bytes 1179656 | tf_op jit(solution)/shard_map/ppermute | solution.py:137
  37.0 2.6 %collective-permute-done.4.x1 = bf16[256,768]{1,0:T(8,128)(2,1)S(1)} collective-permute-done((bf16[256,768]{1,0:T(8,128)(2,1)}, bf16[256,768]{1,0:T(8,128)(2,1)S(1)}, u32[]{:S(2)}, u32[]{:S(2)}) %collective-permute-start.4) | collective-permute-done | bytes 393248 | tf_op jit(solution)/shard_map/ppermute | solution.py:137
  39.6 2.1 %collective-permute-start.5 = (bf16[256,768]{1,0:T(8,128)(2,1)S(1)}, bf16[256,768]{1,0:T(8,128)(2,1)}, u32[]{:S(2)}, u32[]{:S(2)}) collective-permute-start(bf16[256,768]{1,0:T(8,128)(2,1)S(1)} %collective-permute-done.4.x1), channel_id=1, source_target_pairs={{0,1},{1,2},{2,3},{3,4},{4,5},{5,6},{6,7},{7,0},{8,15},{9,8},{10,9... | collective-permute-start | bytes 1179656 | tf_op jit(solution)/shard_map/ppermute | solution.py:137
  41.7 2.7 %collective-permute-done.13.got = bf16[2,96,1024]{2,1,0:T(8,128)(2,1)S(1)} collective-permute-done((bf16[2,96,1024]{2,1,0:T(8,128)(2,1)S(1)}, bf16[2,96,1024]{2,1,0:T(8,128)(2,1)S(1)}, u32[]{:S(2)}, u32[]{:S(2)}) %collective-permute-start.13) | collective-permute-done | bytes 393248 | tf_op jit(solution)/shard_map/ppermute | solution.py:137
  44.5 2.6 %collective-permute-start.14 = (bf16[2,96,1024]{2,1,0:T(8,128)(2,1)S(1)}, bf16[2,96,1024]{2,1,0:T(8,128)(2,1)S(1)}, u32[]{:S(2)}, u32[]{:S(2)}) collective-permute-start(bf16[2,96,1024]{2,1,0:T(8,128)(2,1)S(1)} %shard_map.84), channel_id=1, source_target_pairs={{0,1},{1,2},{2,3},{3,4},{4,5},{5,6},{6,7},{7,0},{8,15},{9,8},{10,9... | collective-permute-start | bytes 1179656 | tf_op jit(solution)/shard_map/ppermute | solution.py:137
  47.1 3.5 %collective-permute-done.5.x2 = bf16[256,768]{1,0:T(8,128)(2,1)} collective-permute-done((bf16[256,768]{1,0:T(8,128)(2,1)S(1)}, bf16[256,768]{1,0:T(8,128)(2,1)}, u32[]{:S(2)}, u32[]{:S(2)}) %collective-permute-start.5) | collective-permute-done | bytes 393248 | tf_op jit(solution)/shard_map/ppermute | solution.py:137
  50.6 1.9 %collective-permute-start.6 = (bf16[256,768]{1,0:T(8,128)(2,1)}, bf16[256,768]{1,0:T(8,128)(2,1)}, u32[]{:S(2)}, u32[]{:S(2)}) collective-permute-start(bf16[256,768]{1,0:T(8,128)(2,1)} %collective-permute-done.5.x2), channel_id=1, source_target_pairs={{0,1},{1,2},{2,3},{3,4},{4,5},{5,6},{6,7},{7,0},{8,15},{9,8},{10,9... | collective-permute-start | bytes 1179656 | tf_op jit(solution)/shard_map/ppermute | solution.py:137
  52.5 2.9 %collective-permute-done.14.got = bf16[2,96,1024]{2,1,0:T(8,128)(2,1)S(1)} collective-permute-done((bf16[2,96,1024]{2,1,0:T(8,128)(2,1)S(1)}, bf16[2,96,1024]{2,1,0:T(8,128)(2,1)S(1)}, u32[]{:S(2)}, u32[]{:S(2)}) %collective-permute-start.14) | collective-permute-done | bytes 393248 | tf_op jit(solution)/shard_map/ppermute | solution.py:137
  56.2 1.9 %collective-permute-start.15 = (bf16[2,96,1024]{2,1,0:T(8,128)(2,1)}, bf16[2,96,1024]{2,1,0:T(8,128)(2,1)S(1)}, u32[]{:S(2)}, u32[]{:S(2)}) collective-permute-start(bf16[2,96,1024]{2,1,0:T(8,128)(2,1)} %shard_map.85), channel_id=1, source_target_pairs={{0,1},{1,2},{2,3},{3,4},{4,5},{5,6},{6,7},{7,0},{8,15},{9,8},{10,9... | collective-permute-start | bytes 1179656 | tf_op jit(solution)/shard_map/ppermute | solution.py:137
  58.1 6.4 %all-to-all-start.2 = ((bf16[8,128,256]{2,1,0:T(8,128)(2,1)}), bf16[8,128,256]{2,1,0:T(8,128)(2,1)S(1)}, u32[]{:S(2)}, u32[]{:S(2)}) async-start(bf16[8,128,256]{2,1,0:T(8,128)(2,1)} %all-to-all-done.1), calls=%async_computation.2 | async-start | bytes 1048576 | tf_op jit(solution)/shard_map/all_to_all | solution.py:162
  64.5 1.9 %collective-permute-start.8 = (bf16[256,768]{1,0:T(8,128)(2,1)}, bf16[256,768]{1,0:T(8,128)(2,1)S(1)}, u32[]{:S(2)}, u32[]{:S(2)}) collective-permute-start(bf16[256,768]{1,0:T(8,128)(2,1)} %copy-done.4), channel_id=1, source_target_pairs={{0,8},{8,0},{1,9},{9,1},{2,10},{10,2},{3,11},{11,3},{4,12},{12,4},... | collective-permute-start | bytes 1179656 | tf_op jit(solution)/shard_map/ppermute | solution.py:138
  66.4 2.4 %collective-permute-start.9 = (bf16[256,768]{1,0:T(8,128)(2,1)}, bf16[256,768]{1,0:T(8,128)(2,1)S(1)}, u32[]{:S(2)}, u32[]{:S(2)}) collective-permute-start(bf16[256,768]{1,0:T(8,128)(2,1)} %collective-permute-done.5.x2), channel_id=1, source_target_pairs={{0,8},{8,0},{1,9},{9,1},{2,10},{10,2},{3,11},{11,3},{4,12},{12,4},... | collective-permute-start | bytes 1179656 | tf_op jit(solution)/shard_map/ppermute | solution.py:138
  68.8 1.9 %collective-permute-start.10 = (bf16[256,768]{1,0:T(8,128)(2,1)}, bf16[256,768]{1,0:T(8,128)(2,1)S(1)}, u32[]{:S(2)}, u32[]{:S(2)}) collective-permute-start(bf16[256,768]{1,0:T(8,128)(2,1)} %collective-permute-done.6.x3), channel_id=1, source_target_pairs={{0,8},{8,0},{1,9},{9,1},{2,10},{10,2},{3,11},{11,3},{4,12},{12,4},... | collective-permute-start | bytes 1179656 | tf_op jit(solution)/shard_map/ppermute | solution.py:138
  70.8 3.9 %collective-permute-start.7 = (bf16[256,768]{1,0:T(8,128)(2,1)}, bf16[256,768]{1,0:T(8,128)(2,1)S(1)}, u32[]{:S(2)}, u32[]{:S(2)}) collective-permute-start(bf16[256,768]{1,0:T(8,128)(2,1)} %collective-permute-done.6.x3), channel_id=1, source_target_pairs={{0,1},{1,2},{2,3},{3,4},{4,5},{5,6},{6,7},{7,0},{8,15},{9,8},{10,9... | collective-permute-start | bytes 1179656 | tf_op jit(solution)/shard_map/ppermute | solution.py:137
  77.6 3.3 %collective-permute-start = (bf16[4,96,256]{2,1,0:T(8,128)(2,1)S(1)}, bf16[4,96,256]{2,1,0:T(8,128)(2,1)S(1)}, u32[]{:S(2)}, u32[]{:S(2)}) collective-permute-start(bf16[4,96,256]{2,1,0:T(8,128)(2,1)S(1)} %shard_map.78), channel_id=1, source_target_pairs={{0,8},{8,0},{1,9},{9,1},{2,10},{10,2},{3,11},{11,3},{4,12},{12,4},... | collective-permute-start | bytes 589832 | tf_op jit(solution)/shard_map/ppermute | solution.py:138
  82.0 2.3 %collective-permute-start.16 = (bf16[96,1024]{1,0:T(8,128)(2,1)S(1)}, bf16[96,1024]{1,0:T(8,128)(2,1)S(1)}, u32[]{:S(2)}, u32[]{:S(2)}) collective-permute-start(bf16[96,1024]{1,0:T(8,128)(2,1)S(1)} %slice_bitcast_fusion), channel_id=1, source_target_pairs={{0,8},{8,0},{1,9},{9,1},{2,10},{10,2},{3,11},{11,3},{4,12},{12,4},... | collective-permute-start | bytes 589832 | tf_op jit(solution)/shard_map/ppermute | solution.py:138
  84.3 1.5 %shard_map.79 = (bf16[96,256]{1,0:T(8,128)(2,1)S(1)}, bf16[96,256]{1,0:T(8,128)(2,1)S(1)}, bf16[96,256]{1,0:T(8,128)(2,1)S(1)}, bf16[96,256]{1,0:T(8,128)(2,1)S(1)}) custom-call(bf16[768,1024]{1,0:T(8,128)(2,1)S(1)} %copy-done.1, bf16[1024,256]{1,0:T(8,128)(2,1)} %bitcast.1.pg, bf16[4,96,256]{2,1,0:T(8,128)(2,1)S(1)} %collective-permute-done.got), custom_call_target="tpu_custom_call" | custom-call | tf_op jit(solution)/shard_map/pallas_call | solution.py:28
  85.8 6.1 %collective-permute-start.1 = (bf16[96,256]{1,0:T(8,128)(2,1)S(1)}, bf16[96,256]{1,0:T(8,128)(2,1)S(1)}, u32[]{:S(2)}, u32[]{:S(2)}) collective-permute-start(bf16[96,256]{1,0:T(8,128)(2,1)S(1)} %get-tuple-element.12), channel_id=1, source_target_pairs={{0,16},{16,32},{32,48},{48,0},{1,17},{17,33},{33,49},{49,1},{2,18}... | collective-permute-start | bytes 147464 | tf_op jit(solution)/shard_map/ppermute | solution.py:167
  91.9 6.1 %collective-permute-done.1.b = bf16[96,256]{1,0:T(8,128)(2,1)S(1)} collective-permute-done((bf16[96,256]{1,0:T(8,128)(2,1)S(1)}, bf16[96,256]{1,0:T(8,128)(2,1)S(1)}, u32[]{:S(2)}, u32[]{:S(2)}) %collective-permute-start.1) | collective-permute-done | bytes 49184 | tf_op jit(solution)/shard_map/ppermute | solution.py:167
  98.0 5.9 %collective-permute-start.2 = (bf16[96,256]{1,0:T(8,128)(2,1)S(1)}, bf16[96,256]{1,0:T(8,128)(2,1)S(1)}, u32[]{:S(2)}, u32[]{:S(2)}) collective-permute-start(bf16[96,256]{1,0:T(8,128)(2,1)S(1)} %get-tuple-element.13), channel_id=1, source_target_pairs={{0,32},{16,48},{32,0},{48,16},{1,33},{17,49},{33,1},{49,17},{2,34}... | collective-permute-start | bytes 147464 | tf_op jit(solution)/shard_map/ppermute | solution.py:167
  103.9 4.5 %collective-permute-done.2.c = bf16[96,256]{1,0:T(8,128)(2,1)S(1)} collective-permute-done((bf16[96,256]{1,0:T(8,128)(2,1)S(1)}, bf16[96,256]{1,0:T(8,128)(2,1)S(1)}, u32[]{:S(2)}, u32[]{:S(2)}) %collective-permute-start.2) | collective-permute-done | bytes 49184 | tf_op jit(solution)/shard_map/ppermute | solution.py:167
  108.4 4.2 %collective-permute-start.3 = (bf16[96,256]{1,0:T(8,128)(2,1)S(1)}, bf16[96,256]{1,0:T(8,128)(2,1)S(1)}, u32[]{:S(2)}, u32[]{:S(2)}) collective-permute-start(bf16[96,256]{1,0:T(8,128)(2,1)S(1)} %get-tuple-element.14), channel_id=1, source_target_pairs={{0,48},{16,0},{32,16},{48,32},{1,49},{17,1},{33,17},{49,33},{2,50}... | collective-permute-start | bytes 147464 | tf_op jit(solution)/shard_map/ppermute | solution.py:167
  113.4 2.4 %collective-permute-done.3.d = bf16[96,256]{1,0:T(8,128)(2,1)S(1)} collective-permute-done((bf16[96,256]{1,0:T(8,128)(2,1)S(1)}, bf16[96,256]{1,0:T(8,128)(2,1)S(1)}, u32[]{:S(2)}, u32[]{:S(2)}) %collective-permute-start.3) | collective-permute-done | bytes 49184 | tf_op jit(solution)/shard_map/ppermute | solution.py:167
  125.5 2.4 %shard_map.81 = bf16[768,128]{1,0:T(8,128)(2,1)} custom-call(bf16[8,128,256]{2,1,0:T(8,128)(2,1)S(1)} %all-to-all-done.2.pg, bf16[256,768]{1,0:T(8,128)(2,1)S(1)} %copy-done.3, bf16[256,768]{1,0:T(8,128)(2,1)S(1)} %copy-done.5, bf16[256,768]{1,0:T(8,128)(2,1)} %collective-permute-done.5.x2, bf16[256,768]{1,0:T(8,128)(2,1)} %collective-permute-done.6.x3, ...), custom_call_target="tpu_custom_call" | custom-call | tf_op jit(solution)/shard_map/pallas_call | solution.py:28
  (58 shorter events, 21.0 us)
Async XLA Ops:
  0.6 1.4 %copy-start = (bf16[1024,768]{1,0:T(8,128)(2,1)S(1)}, bf16[1024,768]{1,0:T(8,128)(2,1)}, u32[]{:S(2)}) copy-start(bf16[1024,768]{1,0:T(8,128)(2,1)} %param.9) | copy-start | bytes 4718596
  0.6 15.0 %copy-start.2 = (bf16[256,768]{1,0:T(8,128)(2,1)S(1)}, bf16[256,768]{1,0:T(8,128)(2,1)}, u32[]{:S(2)}) copy-start(bf16[256,768]{1,0:T(8,128)(2,1)} %out_grad.1) | copy-start | bytes 1179652
  4.4 16.5 %all-to-all-start = ((bf16[8,128,256]{2,1,0:T(8,128)(2,1)}), bf16[8,128,256]{2,1,0:T(8,128)(2,1)S(1)}, u32[]{:S(2)}, u32[]{:S(2)}) async-start(bf16[8,128,256]{2,1,0:T(8,128)(2,1)} %bitcast), calls=%async_computation | async-start | bytes 1048576 | tf_op jit(solution)/shard_map/all_to_all | solution.py:144
  13.7 17.1 %collective-permute-start.12 = (bf16[256,1024]{1,0:T(8,128)(2,1)}, bf16[256,1024]{1,0:T(8,128)(2,1)}, u32[]{:S(2)}, u32[]{:S(2)}) collective-permute-start(bf16[256,1024]{1,0:T(8,128)(2,1)} %pre.1), channel_id=1, source_target_pairs={{0,8},{8,0},{1,9},{9,1},{2,10},{10,2},{3,11},{11,3},{4,12},{12,4},... | collective-permute-start | bytes 1572872 | tf_op jit(solution)/shard_map/ppermute | solution.py:138
  19.0 13.5 %collective-permute-start.11 = (bf16[96,1024]{1,0:T(8,128)(2,1)}, bf16[96,1024]{1,0:T(8,128)(2,1)}, u32[]{:S(2)}, u32[]{:S(2)}) collective-permute-start(bf16[96,1024]{1,0:T(8,128)(2,1)} %slice_bitcast_fusion.1), channel_id=1, source_target_pairs={{0,1},{1,2},{2,3},{3,4},{4,5},{5,6},{6,7},{7,0},{8,15},{9,8},{10,9... | collective-permute-start | bytes 589832 | tf_op jit(solution)/shard_map/ppermute | solution.py:137
  20.9 10.0 %copy-start.15 = (bf16[768,256]{1,0:T(8,128)(2,1)S(1)}, bf16[768,256]{1,0:T(8,128)(2,1)}, u32[]{:S(2)}) copy-start(bf16[768,256]{1,0:T(8,128)(2,1)} %copy-done.14) | copy-start | bytes 1179652
  21.0 1.0 copy-start.17
  22.8 35.3 %all-to-all-start.1 = ((bf16[8,128,256]{2,1,0:T(8,128)(2,1)}), bf16[8,128,256]{2,1,0:T(8,128)(2,1)}, u32[]{:S(2)}, u32[]{:S(2)}) async-start(bf16[8,128,256]{2,1,0:T(8,128)(2,1)} %shard_map.77), calls=%async_computation.1 | async-start | bytes 1048576 | tf_op jit(solution)/shard_map/all_to_all | solution.py:156
  28.5 11.1 %collective-permute-start.4 = (bf16[256,768]{1,0:T(8,128)(2,1)}, bf16[256,768]{1,0:T(8,128)(2,1)S(1)}, u32[]{:S(2)}, u32[]{:S(2)}) collective-permute-start(bf16[256,768]{1,0:T(8,128)(2,1)} %x0.1), channel_id=1, source_target_pairs={{0,1},{1,2},{2,3},{3,4},{4,5},{5,6},{6,7},{7,0},{8,15},{9,8},{10,9... | collective-permute-start | bytes 1179656 | tf_op jit(solution)/shard_map/ppermute | solution.py:137
  33.5 10.9 %collective-permute-start.13 = (bf16[2,96,1024]{2,1,0:T(8,128)(2,1)S(1)}, bf16[2,96,1024]{2,1,0:T(8,128)(2,1)S(1)}, u32[]{:S(2)}, u32[]{:S(2)}) collective-permute-start(bf16[2,96,1024]{2,1,0:T(8,128)(2,1)S(1)} %shard_map.83), channel_id=1, source_target_pairs={{0,1},{1,2},{2,3},{3,4},{4,5},{5,6},{6,7},{7,0},{8,15},{9,8},{10,9... | collective-permute-start | bytes 1179656 | tf_op jit(solution)/shard_map/ppermute | solution.py:137
  39.6 16.6 %copy-start.4 = (bf16[256,768]{1,0:T(8,128)(2,1)}, bf16[256,768]{1,0:T(8,128)(2,1)S(1)}, u32[]{:S(2)}) copy-start(bf16[256,768]{1,0:T(8,128)(2,1)S(1)} %collective-permute-done.4.x1) | copy-start | bytes 1179652
  39.6 11.0 %collective-permute-start.5 = (bf16[256,768]{1,0:T(8,128)(2,1)S(1)}, bf16[256,768]{1,0:T(8,128)(2,1)}, u32[]{:S(2)}, u32[]{:S(2)}) collective-permute-start(bf16[256,768]{1,0:T(8,128)(2,1)S(1)} %collective-permute-done.4.x1), channel_id=1, source_target_pairs={{0,1},{1,2},{2,3},{3,4},{4,5},{5,6},{6,7},{7,0},{8,15},{9,8},{10,9... | collective-permute-start | bytes 1179656 | tf_op jit(solution)/shard_map/ppermute | solution.py:137
  44.5 10.9 %collective-permute-start.14 = (bf16[2,96,1024]{2,1,0:T(8,128)(2,1)S(1)}, bf16[2,96,1024]{2,1,0:T(8,128)(2,1)S(1)}, u32[]{:S(2)}, u32[]{:S(2)}) collective-permute-start(bf16[2,96,1024]{2,1,0:T(8,128)(2,1)S(1)} %shard_map.84), channel_id=1, source_target_pairs={{0,1},{1,2},{2,3},{3,4},{4,5},{5,6},{6,7},{7,0},{8,15},{9,8},{10,9... | collective-permute-start | bytes 1179656 | tf_op jit(solution)/shard_map/ppermute | solution.py:137
  50.6 18.3 %collective-permute-start.6 = (bf16[256,768]{1,0:T(8,128)(2,1)}, bf16[256,768]{1,0:T(8,128)(2,1)}, u32[]{:S(2)}, u32[]{:S(2)}) collective-permute-start(bf16[256,768]{1,0:T(8,128)(2,1)} %collective-permute-done.5.x2), channel_id=1, source_target_pairs={{0,1},{1,2},{2,3},{3,4},{4,5},{5,6},{6,7},{7,0},{8,15},{9,8},{10,9... | collective-permute-start | bytes 1179656 | tf_op jit(solution)/shard_map/ppermute | solution.py:137
  56.2 21.4 %collective-permute-start.15 = (bf16[2,96,1024]{2,1,0:T(8,128)(2,1)}, bf16[2,96,1024]{2,1,0:T(8,128)(2,1)S(1)}, u32[]{:S(2)}, u32[]{:S(2)}) collective-permute-start(bf16[2,96,1024]{2,1,0:T(8,128)(2,1)} %shard_map.85), channel_id=1, source_target_pairs={{0,1},{1,2},{2,3},{3,4},{4,5},{5,6},{6,7},{7,0},{8,15},{9,8},{10,9... | collective-permute-start | bytes 1179656 | tf_op jit(solution)/shard_map/ppermute | solution.py:137
  58.1 61.3 %all-to-all-start.2 = ((bf16[8,128,256]{2,1,0:T(8,128)(2,1)}), bf16[8,128,256]{2,1,0:T(8,128)(2,1)S(1)}, u32[]{:S(2)}, u32[]{:S(2)}) async-start(bf16[8,128,256]{2,1,0:T(8,128)(2,1)} %all-to-all-done.1), calls=%async_computation.2 | async-start | bytes 1048576 | tf_op jit(solution)/shard_map/all_to_all | solution.py:162
  64.5 52.0 %collective-permute-start.8 = (bf16[256,768]{1,0:T(8,128)(2,1)}, bf16[256,768]{1,0:T(8,128)(2,1)S(1)}, u32[]{:S(2)}, u32[]{:S(2)}) collective-permute-start(bf16[256,768]{1,0:T(8,128)(2,1)} %copy-done.4), channel_id=1, source_target_pairs={{0,8},{8,0},{1,9},{9,1},{2,10},{10,2},{3,11},{11,3},{4,12},{12,4},... | collective-permute-start | bytes 1179656 | tf_op jit(solution)/shard_map/ppermute | solution.py:138
  66.4 50.8 %collective-permute-start.9 = (bf16[256,768]{1,0:T(8,128)(2,1)}, bf16[256,768]{1,0:T(8,128)(2,1)S(1)}, u32[]{:S(2)}, u32[]{:S(2)}) collective-permute-start(bf16[256,768]{1,0:T(8,128)(2,1)} %collective-permute-done.5.x2), channel_id=1, source_target_pairs={{0,8},{8,0},{1,9},{9,1},{2,10},{10,2},{3,11},{11,3},{4,12},{12,4},... | collective-permute-start | bytes 1179656 | tf_op jit(solution)/shard_map/ppermute | solution.py:138
  68.8 49.1 %collective-permute-start.10 = (bf16[256,768]{1,0:T(8,128)(2,1)}, bf16[256,768]{1,0:T(8,128)(2,1)S(1)}, u32[]{:S(2)}, u32[]{:S(2)}) collective-permute-start(bf16[256,768]{1,0:T(8,128)(2,1)} %collective-permute-done.6.x3), channel_id=1, source_target_pairs={{0,8},{8,0},{1,9},{9,1},{2,10},{10,2},{3,11},{11,3},{4,12},{12,4},... | collective-permute-start | bytes 1179656 | tf_op jit(solution)/shard_map/ppermute | solution.py:138
  70.8 48.0 %collective-permute-start.7 = (bf16[256,768]{1,0:T(8,128)(2,1)}, bf16[256,768]{1,0:T(8,128)(2,1)S(1)}, u32[]{:S(2)}, u32[]{:S(2)}) collective-permute-start(bf16[256,768]{1,0:T(8,128)(2,1)} %collective-permute-done.6.x3), channel_id=1, source_target_pairs={{0,1},{1,2},{2,3},{3,4},{4,5},{5,6},{6,7},{7,0},{8,15},{9,8},{10,9... | collective-permute-start | bytes 1179656 | tf_op jit(solution)/shard_map/ppermute | solution.py:137
  74.7 1.4 %copy-start.1 = (bf16[768,1024]{1,0:T(8,128)(2,1)S(1)}, bf16[768,1024]{1,0:T(8,128)(2,1)}, u32[]{:S(2)}) copy-start(bf16[768,1024]{1,0:T(8,128)(2,1)} %w.3) | copy-start | bytes 4718596
  77.6 4.4 %collective-permute-start = (bf16[4,96,256]{2,1,0:T(8,128)(2,1)S(1)}, bf16[4,96,256]{2,1,0:T(8,128)(2,1)S(1)}, u32[]{:S(2)}, u32[]{:S(2)}) collective-permute-start(bf16[4,96,256]{2,1,0:T(8,128)(2,1)S(1)} %shard_map.78), channel_id=1, source_target_pairs={{0,8},{8,0},{1,9},{9,1},{2,10},{10,2},{3,11},{11,3},{4,12},{12,4},... | collective-permute-start | bytes 589832 | tf_op jit(solution)/shard_map/ppermute | solution.py:138
  82.0 3.8 %collective-permute-start.16 = (bf16[96,1024]{1,0:T(8,128)(2,1)S(1)}, bf16[96,1024]{1,0:T(8,128)(2,1)S(1)}, u32[]{:S(2)}, u32[]{:S(2)}) collective-permute-start(bf16[96,1024]{1,0:T(8,128)(2,1)S(1)} %slice_bitcast_fusion), channel_id=1, source_target_pairs={{0,8},{8,0},{1,9},{9,1},{2,10},{10,2},{3,11},{11,3},{4,12},{12,4},... | collective-permute-start | bytes 589832 | tf_op jit(solution)/shard_map/ppermute | solution.py:138
  85.8 12.2 %collective-permute-start.1 = (bf16[96,256]{1,0:T(8,128)(2,1)S(1)}, bf16[96,256]{1,0:T(8,128)(2,1)S(1)}, u32[]{:S(2)}, u32[]{:S(2)}) collective-permute-start(bf16[96,256]{1,0:T(8,128)(2,1)S(1)} %get-tuple-element.12), channel_id=1, source_target_pairs={{0,16},{16,32},{32,48},{48,0},{1,17},{17,33},{33,49},{49,1},{2,18}... | collective-permute-start | bytes 147464 | tf_op jit(solution)/shard_map/ppermute | solution.py:167
  98.0 10.4 %collective-permute-start.2 = (bf16[96,256]{1,0:T(8,128)(2,1)S(1)}, bf16[96,256]{1,0:T(8,128)(2,1)S(1)}, u32[]{:S(2)}, u32[]{:S(2)}) collective-permute-start(bf16[96,256]{1,0:T(8,128)(2,1)S(1)} %get-tuple-element.13), channel_id=1, source_target_pairs={{0,32},{16,48},{32,0},{48,16},{1,33},{17,49},{33,1},{49,17},{2,34}... | collective-permute-start | bytes 147464 | tf_op jit(solution)/shard_map/ppermute | solution.py:167
  108.4 7.4 %collective-permute-start.3 = (bf16[96,256]{1,0:T(8,128)(2,1)S(1)}, bf16[96,256]{1,0:T(8,128)(2,1)S(1)}, u32[]{:S(2)}, u32[]{:S(2)}) collective-permute-start(bf16[96,256]{1,0:T(8,128)(2,1)S(1)} %get-tuple-element.14), channel_id=1, source_target_pairs={{0,48},{16,0},{32,16},{48,32},{1,49},{17,1},{33,17},{49,33},{2,50}... | collective-permute-start | bytes 147464 | tf_op jit(solution)/shard_map/ppermute | solution.py:167
  119.5 1.0 copy-start.3
  120.5 1.0 copy-start.5
  121.5 1.0 copy-start.7
  122.5 1.0 copy-start.9
  123.5 1.0 copy-start.11
  124.5 1.0 copy-start.13
  (6 other events, 4.5 us)

commit v3 on v0

v3 whole, which is shorter than its diff:
```python
import functools
import math

import jax
import jax.numpy as jnp
from jax import lax
from jax.experimental import pallas as pl
from jax.experimental.pallas import tpu as pltpu
from jax.sharding import Mesh, PartitionSpec as P

BF = jnp.bfloat16
F32 = jnp.float32
IN = ("x", "zlo")
OUT = ("zhi", "core")
SWAP = [(0, 1), (1, 0)]
N = 8


def sds(shape, dtype=BF):
    return jax.ShapeDtypeStruct(shape, dtype)


def call(body, outs, *args, scratch=(), flops=0, touched=0, hold=0):
    vm = pl.BlockSpec(memory_space=pltpu.VMEM)
    many = isinstance(outs, (list, tuple))
    return pl.pallas_call(
        body,
        out_shape=outs,
        in_specs=[vm] * (len(args) - hold) + [pl.BlockSpec(memory_space=pl.ANY)] * hold,
        out_specs=[vm] * len(outs) if many else vm,
        scratch_shapes=list(scratch),
        compiler_params=pltpu.CompilerParams(vmem_limit_bytes=60 * 1024 * 1024),
        cost_estimate=pl.CostEstimate(flops=flops, bytes_accessed=touched, transcendentals=0),
    )(*args)


def cdf_of(value):
    return 0.5 * (1.0 + lax.erf(value * 0.7071067811865476))


def density_of(value):
    return jnp.exp(-0.5 * value * value) * 0.3989422804014327


def dot(a, b):
    return jnp.dot(a, b, preferred_element_type=F32)


def out_terms(factor, out_grad, pre, term, deriv, turned):
    v = pre[...].astype(F32)
    act = (v * cdf_of(v)).astype(BF)
    turned[...] = out_grad[...].T
    width = turned.shape[0] // N
    for k in range(N):
        part = slice(k * width, (k + 1) * width)
        term[part, :] = (dot(turned[part, :], act) * factor).astype(BF)
    rows = pre.shape[0] // N
    i = lax.axis_index(IN)
    u = pre[pl.ds(pl.multiple_of(i * rows, rows), rows), :].astype(F32)
    deriv[...] = cdf_of(u) + u * density_of(u)


def note(flops, *made):
    def body(*refs):
        refs[-1][0, 0] = 0

    return pl.pallas_call(
        body,
        out_shape=sds((1, 1), jnp.int32),
        in_specs=[pl.BlockSpec(memory_space=pl.ANY)] * len(made),
        out_specs=pl.BlockSpec(memory_space=pltpu.SMEM),
        compiler_params=pltpu.CompilerParams(vmem_limit_bytes=60 * 1024 * 1024),
        cost_estimate=pl.CostEstimate(flops=flops, bytes_accessed=0, transcendentals=0),
    )(*made)


def weight_grad(factor, recv, x0, x1, x2, x3, x4, z1, z2, z3, step, step2, step3, out):
    y = lax.axis_index("batch")
    s = 1 - 2 * lax.axis_index("core")
    rows = x0.shape[0] // N
    total = jnp.zeros((out.shape[1], out.shape[0]), F32)
    for k, ref in ((0, x0), (-1, x1), (-2, x2), (-3, x3), (4, x4), (1, z1), (2, z2), (3, z3)):
        at = pl.multiple_of(((y + s * k + N) % N) * rows, rows)
        block = jnp.concatenate([recv[i, pl.ds(at, rows), :] for i in range(N)], 0)
        total = total + dot(block.T, ref[...])
    out[...] = (total * factor).T.astype(BF)


def per_device(inputs, out_grad, pre_act, w_in, w_out):
    tok, d_in = inputs.shape
    hid = pre_act.shape[1]
    factor = 1.0 / math.sqrt(tok * N)
    piece, wide, rows = d_in // N, hid // N, tok // N
    core = lax.axis_index("core")
    scope = jax.named_scope
    fence = lax.optimization_barrier

    def away(a, step, name):
        with scope(name):
            pairs = [(b, (b + step) % N) for b in range(N)]
            pairs += [(N + b, N + (b - step) % N) for b in range(N)]
            return lax.ppermute(a, ("core", "batch"), pairs)

    def swap(a, name):
        with scope(name):
            return lax.ppermute(a, "core", SWAP)

    def spread(a, axis, name):
        with scope(name):
            return lax.all_to_all(a, axis, 0, 0, tiled=True)

    with scope("partial"):
        part = lax.dot_general(out_grad, w_out, (((1,), (1,)), ((), ())), preferred_element_type=F32)
        part = part.astype(BF).reshape(N, rows, hid)
    got = spread(part, IN, "hidden_reduce")
    x1 = away(inputs, 1, "x1")
    with scope("out_terms"):
        w_out_term, deriv = call(
            functools.partial(out_terms, factor),
            [sds((d_in, hid)), sds((rows, hid), F32)],
            out_grad,
            pre_act,
            scratch=[pltpu.VMEM((d_in, tok), BF)],
        )
    with scope("w_out_sum"):
        w_out_grad = lax.psum_scatter(w_out_term, "batch", scatter_dimension=0, tiled=True).T

    with scope("hidden_grad"):
        total = jnp.sum(got.astype(F32), axis=0)
        mine = (total * deriv).astype(BF)
    mine, w_out_term = fence((mine, w_out_term))
    with scope("hidden_copy"):
        copies = jnp.broadcast_to(mine, (N, rows, hid))
    pg = spread(copies, IN, "hidden_spread").reshape(tok, hid)
    with scope("hidden_blocks"):
        blocks = mine.reshape(rows, N, wide).swapaxes(0, 1)
    x2 = away(x1, 1, "x2")
    z1 = swap(x1, "z1")
    with scope("step"):
        step = note(3000000000, z1)
    pg, blocks, step = fence((pg, blocks, step))
    across = spread(blocks, "batch", "batch_spread")

    with scope("input_term"):
        term = lax.dot_general(w_in, pg, (((1,), (1,)), ((), ())), preferred_element_type=F32)
        term = term.astype(BF).reshape(4, 2, piece, tok)
    with scope("send_half"):
        far_half = lax.dynamic_index_in_dim(term, 1 - core, 1, False)
    got_half = swap(far_half, "half_swap")
    far_half, x2 = fence((far_half, x2))
    x3 = away(x2, 1, "x3")
    z2 = swap(x2, "z2")
    with scope("keep_half"):
        near = lax.dynamic_index_in_dim(term, core, 1, False)
        kept = (near.astype(F32) + got_half.astype(F32)).astype(BF)
    with scope("step2"):
        step2 = note(3000000000, across)
    across, step2 = fence((across, step2))
    with scope("across_copy"):
        copies = jnp.broadcast_to(across, (N, N, rows, wide))
    recv = spread(copies, IN, "across_spread").reshape(N, tok, wide)
    x4 = away(x3, 1, "x4")
    z3 = swap(x3, "z3")
    with scope("step3"):
        step3 = note(6000000000, x3)
    recv, kept, step3 = fence((recv, kept, step3))
    quad = spread(kept, "zhi", "zhi_spread")
    with scope("weight_grad"):
        w_in_grad = call(
            functools.partial(weight_grad, factor),
            sds((d_in, wide)),
            recv, inputs, x1, x2, x3, x4, z1, z2, z3, step, step2, step3,
            hold=3,
        )
    quad, w_in_grad = fence((quad, w_in_grad))
    with scope("sum_four"):
        input_grad = jnp.sum(quad.astype(F32), axis=0).astype(BF).T
    return (input_grad, w_in_grad, w_out_grad)


def solution(mesh):
    fine = Mesh(mesh.devices.reshape(4, 2, 4, 2, 8), ("x", "zlo", "zhi", "core", "batch"))
    return jax.shard_map(
        per_device,
        mesh=fine,
        in_specs=(P("batch", IN), P("batch", IN), P("batch", OUT), P(IN, OUT), P(OUT, IN)),
        out_specs=(P("batch", IN + OUT), P(IN, OUT + ("batch",)), P(OUT, IN + ("batch",))),
        check_vma=False,
    )
```

time: 241 us -> 102 us (0.42)
  the two profiles are of different devices: /device:TPU:1 before, /device:TPU:2 now
where the time goes in v3:
time: 102 us; the launch traced here: 101 us
  starting transfers between devices  53.9 us (53%)
  between operations  14.3 us (14%)
  Pallas kernels  10.2 us (10%)
  waiting for transfers between devices  8.42 us (8%)
  local copies, waits for them, and re-layouts  6.98 us (7%)
  matrix products  4.45 us (4%)
  other arithmetic  2.41 us (2%)
    all_to_all x5, starting transfers between devices, spread(): return lax.all_to_all(a, axis, 0, 0, tiled=True)  34.9 us
    ppermute x4, starting transfers between devices, away(): return lax.ppermute(a, ('core', 'batch'), pairs)  10.8 us
    pallas_call x2, Pallas kernels, call(): pl.pallas_call(body, out_shape=outs, in_specs=[vm] * (len(args) - hold) +...  8.68 us
    all_to_all x5, waiting for transfers between devices, spread(): return lax.all_to_all(a, axis, 0, 0, tiled=True)  8.38 us
    ppermute x4, starting transfers between devices, swap(): return lax.ppermute(a, 'core', SWAP)  8.14 us
    unnamed x18, local copies, waits for them, and re-layouts  3.53 us
    dot_general x1, matrix products, per_device(): lax.dot_general(out_grad, w_out, (((1,), (1,)), ((), ())), preferred_elem...  2.41 us
  transfers between devices with their start and end apart: 14, of which 4 were waited for; matrix products, arithmetic and copies ran while one was open for 8% of the time, Pallas kernels for 10%

profile of v3, /device:TPU:2, one launch (start us, length us, event | category | flops | bytes accessed | tf_op | source)
XLA Modules:
  0.0 100.6 jit_solution(17182253056833809519)
XLA Ops:
  7.2 1.4 %copy-done = bf16[1024,768]{1,0:T(8,128)(2,1)S(1)} copy-done((bf16[1024,768]{1,0:T(8,128)(2,1)S(1)}, bf16[1024,768]{1,0:T(8,128)(2,1)}, u32[]{:S(2)}) %copy-start) | copy-done | bytes 1572888
  8.6 2.4 %convolution_convert_fusion = bf16[256,1024]{1,0:T(8,128)(2,1)} fusion(bf16[256,768]{1,0:T(8,128)(2,1)} %out_grad.1, bf16[1024,768]{1,0:T(8,128)(2,1)S(1)} %copy-done), kind=kOutput, calls=%fused_computation | convolution fusion | flops 402915328 | bytes 2490368 | tf_op jit(solution)/shard_map/partial/dot_general | solution.py:113
  11.0 9.3 %all-to-all-start = ((bf16[8,32,1024]{2,1,0:T(8,128)(2,1)}), bf16[8,32,1024]{2,1,0:T(8,128)(2,1)S(1)}, u32[]{:S(2)}, u32[]{:S(2)}) async-start(bf16[8,32,1024]{2,1,0:T(8,128)(2,1)} %bitcast), calls=%async_computation | async-start | bytes 1048576 | tf_op jit(solution)/shard_map/hidden_reduce/all_to_all | solution.py:110
  20.3 1.9 %collective-permute-start = (bf16[256,768]{1,0:T(8,128)(2,1)S(1)}, bf16[256,768]{1,0:T(8,128)(2,1)S(1)}, u32[]{:S(2)}, u32[]{:S(2)}) collective-permute-start(bf16[256,768]{1,0:T(8,128)(2,1)S(1)} %copy-done.2), channel_id=1, source_target_pairs={{0,1},{1,2},{2,3},{3,4},{4,5},{5,6},{6,7},{7,0},{8,15},{9,8},{10,9... | collective-permute-start | bytes 1179656 | tf_op jit(solution)/shard_map/x1/ppermute | solution.py:102
  22.2 3.4 %out_terms.1 = (bf16[768,1024]{1,0:T(8,128)(2,1)}, f32[32,1024]{1,0:T(8,128)}) custom-call(bf16[256,768]{1,0:T(8,128)(2,1)} %out_grad.1, bf16[256,1024]{1,0:T(8,128)(2,1)} %pre.1), custom_call_target="tpu_custom_call" | custom-call | tf_op jit(solution)/shard_map/out_terms/pallas_call | solution.py:26
  25.6 1.5 %all-to-all-done = bf16[8,32,1024]{2,1,0:T(8,128)(2,1)S(1)} async-done(((bf16[8,32,1024]{2,1,0:T(8,128)(2,1)}), bf16[8,32,1024]{2,1,0:T(8,128)(2,1)S(1)}, u32[]{:S(2)}, u32[]{:S(2)}) %all-to-all-start) | async-done | bytes 524320 | tf_op jit(solution)/shard_map/hidden_reduce/all_to_all | solution.py:110
  27.3 0.9 broadcast_in_dim.6
  28.1 5.3 %all-to-all-start.1 = ((bf16[8,32,1024]{2,1,0:T(8,128)(2,1)}), bf16[8,32,1024]{2,1,0:T(8,128)(2,1)S(1)}, u32[]{:S(2)}, u32[]{:S(2)}) async-start(bf16[8,32,1024]{2,1,0:T(8,128)(2,1)} %broadcast_in_dim.6), calls=%async_computation.1 | async-start | bytes 1048576 | tf_op jit(solution)/shard_map/hidden_spread/all_to_all | solution.py:110
  33.4 1.9 %collective-permute-start.1 = (bf16[256,768]{1,0:T(8,128)(2,1)S(1)}, bf16[256,768]{1,0:T(8,128)(2,1)S(1)}, u32[]{:S(2)}, u32[]{:S(2)}) collective-permute-start(bf16[256,768]{1,0:T(8,128)(2,1)S(1)} %collective-permute-done.x1), channel_id=1, source_target_pairs={{0,8},{8,0},{1,9},{9,1},{2,10},{10,2},{3,11},{11,3},{4,12},{12,4},... | collective-permute-start | bytes 1179656 | tf_op jit(solution)/shard_map/z1/ppermute | solution.py:106
  35.4 2.2 %collective-permute-start.3 = (bf16[256,768]{1,0:T(8,128)(2,1)S(1)}, bf16[256,768]{1,0:T(8,128)(2,1)}, u32[]{:S(2)}, u32[]{:S(2)}) collective-permute-start(bf16[256,768]{1,0:T(8,128)(2,1)S(1)} %collective-permute-done.x1), channel_id=1, source_target_pairs={{0,1},{1,2},{2,3},{3,4},{4,5},{5,6},{6,7},{7,0},{8,15},{9,8},{10,9... | collective-permute-start | bytes 1179656 | tf_op jit(solution)/shard_map/x2/ppermute | solution.py:102
  37.6 0.7 copy-done.4
  38.3 0.5 step.1
  38.8 0.6 bitcast_bitcast_fusion
  39.5 1.8 %all-to-all-done.1 = bf16[8,32,1024]{2,1,0:T(8,128)(2,1)S(1)} async-done(((bf16[8,32,1024]{2,1,0:T(8,128)(2,1)}), bf16[8,32,1024]{2,1,0:T(8,128)(2,1)S(1)}, u32[]{:S(2)}, u32[]{:S(2)}) %all-to-all-start.1) | async-done | bytes 524320 | tf_op jit(solution)/shard_map/hidden_spread/all_to_all | solution.py:110
  41.3 5.3 %all-to-all-start.2 = ((bf16[8,32,128]{2,1,0:T(8,128)(2,1)}), bf16[8,32,128]{2,1,0:T(8,128)(2,1)S(1)}, u32[]{:S(2)}, u32[]{:S(2)}) async-start(bf16[8,32,128]{2,1,0:T(8,128)(2,1)} %bitcast_bitcast_fusion), calls=%async_computation.2 | async-start | bytes 131072 | tf_op jit(solution)/shard_map/batch_spread/all_to_all | solution.py:110
  46.5 2.0 %fusion = bf16[768,256]{0,1:T(8,128)(2,1)S(1)} fusion(bf16[256,1024]{1,0:T(8,128)(2,1)S(1)} %bitcast.27, bf16[768,1024]{1,0:T(8,128)(2,1)} %param.8), kind=kOutput, calls=%fused_computation.2 | convolution fusion | flops 402849792 | bytes 2490368 | tf_op jit(solution)/shard_map/input_term/dot_general | solution.py:145
  48.8 1.9 %collective-permute-start.2 = (bf16[4,96,256]{2,1,0:T(8,128)(2,1)S(1)}, bf16[4,96,256]{2,1,0:T(8,128)(2,1)}, u32[]{:S(2)}, u32[]{:S(2)}) collective-permute-start(bf16[4,96,256]{2,1,0:T(8,128)(2,1)S(1)} %dynamic-slice_bitcast_fusion), channel_id=1, source_target_pairs={{0,8},{8,0},{1,9},{9,1},{2,10},{10,2},{3,11},{11,3},{4,12},{12,4},... | collective-permute-start | bytes 589832 | tf_op jit(solution)/shard_map/half_swap/ppermute | solution.py:106
  50.7 3.9 %collective-permute-start.4 = (bf16[256,768]{1,0:T(8,128)(2,1)}, bf16[256,768]{1,0:T(8,128)(2,1)S(1)}, u32[]{:S(2)}, u32[]{:S(2)}) collective-permute-start(bf16[256,768]{1,0:T(8,128)(2,1)} %collective-permute-done.3.x2), channel_id=1, source_target_pairs={{0,1},{1,2},{2,3},{3,4},{4,5},{5,6},{6,7},{7,0},{8,15},{9,8},{10,9... | collective-permute-start | bytes 1179656 | tf_op jit(solution)/shard_map/x3/ppermute | solution.py:102
  54.7 0.6 all-to-all-done.2.refs_0_
  55.2 0.6 copy-done.7
  56.4 1.7 %broadcast_in_dim.7 = bf16[8,8,32,128]{3,2,1,0:T(8,128)(2,1)} broadcast(bf16[8,32,128]{2,1,0:T(8,128)(2,1)} %copy-done.7), dimensions={1,2,3} | broadcast | bytes 589824 | tf_op jit(solution)/shard_map/across_copy/broadcast_in_dim | solution.py:160
  58.1 5.4 %all-to-all-start.3 = ((bf16[8,8,32,128]{3,2,1,0:T(8,128)(2,1)}), bf16[8,8,32,128]{3,2,1,0:T(8,128)(2,1)S(1)}, u32[]{:S(2)}, u32[]{:S(2)}) async-start(bf16[8,8,32,128]{3,2,1,0:T(8,128)(2,1)} %broadcast_in_dim.7), calls=%async_computation.3 | async-start | bytes 1048576 | tf_op jit(solution)/shard_map/across_spread/all_to_all | solution.py:110
  63.5 2.4 %collective-permute-start.6 = (bf16[256,768]{1,0:T(8,128)(2,1)}, bf16[256,768]{1,0:T(8,128)(2,1)S(1)}, u32[]{:S(2)}, u32[]{:S(2)}) collective-permute-start(bf16[256,768]{1,0:T(8,128)(2,1)} %collective-permute-done.3.x2), channel_id=1, source_target_pairs={{0,8},{8,0},{1,9},{9,1},{2,10},{10,2},{3,11},{11,3},{4,12},{12,4},... | collective-permute-start | bytes 1179656 | tf_op jit(solution)/shard_map/z2/ppermute | solution.py:106
  65.9 1.7 %fusion.1 = bf16[4,96,256]{2,1,0:T(8,128)(2,1)} fusion(bf16[4,96,256]{2,1,0:T(8,128)(2,1)} %collective-permute-done.2, bf16[4,2,96,256]{3,2,1,0:T(8,128)(2,1)S(1)} %bitcast.26, s32[]{:T(128)S(6)} %select_n.7), kind=kLoop, calls=%fused_computation.5 | loop fusion | flops 393216 | bytes 589828 | tf_op jit(solution)/shard_map/keep_half/convert_element_type | solution.py:155
  67.6 1.9 %collective-permute-start.7 = (bf16[256,768]{1,0:T(8,128)(2,1)S(1)}, bf16[256,768]{1,0:T(8,128)(2,1)}, u32[]{:S(2)}, u32[]{:S(2)}) collective-permute-start(bf16[256,768]{1,0:T(8,128)(2,1)S(1)} %collective-permute-done.4.refs_0_.x3), channel_id=1, source_target_pairs={{0,8},{8,0},{1,9},{9,1},{2,10},{10,2},{3,11},{11,3},{4,12},{12,4},... | collective-permute-start | bytes 1179656 | tf_op jit(solution)/shard_map/z3/ppermute | solution.py:106
  69.5 2.8 %collective-permute-start.5 = (bf16[256,768]{1,0:T(8,128)(2,1)S(1)}, bf16[256,768]{1,0:T(8,128)(2,1)}, u32[]{:S(2)}, u32[]{:S(2)}) collective-permute-start(bf16[256,768]{1,0:T(8,128)(2,1)S(1)} %collective-permute-done.4.refs_0_.x3), channel_id=1, source_target_pairs={{0,1},{1,2},{2,3},{3,4},{4,5},{5,6},{6,7},{7,0},{8,15},{9,8},{10,9... | collective-permute-start | bytes 1179656 | tf_op jit(solution)/shard_map/x4/ppermute | solution.py:102
  72.3 0.5 step3.1
  72.9 9.7 %all-to-all-start.4 = ((bf16[4,96,256]{2,1,0:T(8,128)(2,1)}), bf16[4,96,256]{2,1,0:T(8,128)(2,1)S(1)}, u32[]{:S(2)}, u32[]{:S(2)}) async-start(bf16[4,96,256]{2,1,0:T(8,128)(2,1)} %fusion.1), calls=%async_computation.4 | async-start | bytes 393216 | tf_op jit(solution)/shard_map/zhi_spread/all_to_all | solution.py:110
  82.6 0.8 copy-done.6
  83.3 5.3 %weight_grad.1 = bf16[768,128]{1,0:T(8,128)(2,1)} custom-call(bf16[8,256,128]{2,1,0:T(8,128)(2,1)} %bitcast.24, bf16[256,768]{1,0:T(8,128)(2,1)} %x0.1, bf16[256,768]{1,0:T(8,128)(2,1)} %copy-done.3, bf16[256,768]{1,0:T(8,128)(2,1)} %collective-permute-done.3.x2, bf16[256,768]{1,0:T(8,128)(2,1)} %copy-done.5, bf16[256,768]{1,0:T(8,128)(2,1)} %collective-permute-done.5.x4, ...), custom_call_target="tpu_custom_call" | custom-call | tf_op jit(solution)/shard_map/weight_grad/pallas_call | solution.py:26
  88.6 4.5 %all-to-all-done.4 = bf16[4,96,256]{2,1,0:T(8,128)(2,1)S(1)} async-done(((bf16[4,96,256]{2,1,0:T(8,128)(2,1)}), bf16[4,96,256]{2,1,0:T(8,128)(2,1)S(1)}, u32[]{:S(2)}, u32[]{:S(2)}) %all-to-all-start.4) | async-done | bytes 196640 | tf_op jit(solution)/shard_map/zhi_spread/all_to_all | solution.py:110
  93.1 0.7 reduce_sum.22
  (31 shorter events, 0.9 us)
Async XLA Ops:
  7.2 1.4 %copy-start = (bf16[1024,768]{1,0:T(8,128)(2,1)S(1)}, bf16[1024,768]{1,0:T(8,128)(2,1)}, u32[]{:S(2)}) copy-start(bf16[1024,768]{1,0:T(8,128)(2,1)} %param.9) | copy-start | bytes 4718596
  7.2 13.1 %copy-start.2 = (bf16[256,768]{1,0:T(8,128)(2,1)S(1)}, bf16[256,768]{1,0:T(8,128)(2,1)}, u32[]{:S(2)}) copy-start(bf16[256,768]{1,0:T(8,128)(2,1)} %x0.1) | copy-start | bytes 1179652
  11.0 16.2 %all-to-all-start = ((bf16[8,32,1024]{2,1,0:T(8,128)(2,1)}), bf16[8,32,1024]{2,1,0:T(8,128)(2,1)S(1)}, u32[]{:S(2)}, u32[]{:S(2)}) async-start(bf16[8,32,1024]{2,1,0:T(8,128)(2,1)} %bitcast), calls=%async_computation | async-start | bytes 1048576 | tf_op jit(solution)/shard_map/hidden_reduce/all_to_all | solution.py:110
  20.3 73.5 %reduce-scatter.2.cloned.1.call-start = ((), (), s32[]{:S(2)}) async-start(), calls=%async_computation.6 | async-start | bytes 1769472 | tf_op jit(solution)/shard_map/w_out_sum/reduce_scatter | solution.py:126
  20.3 13.1 %collective-permute-start = (bf16[256,768]{1,0:T(8,128)(2,1)S(1)}, bf16[256,768]{1,0:T(8,128)(2,1)S(1)}, u32[]{:S(2)}, u32[]{:S(2)}) collective-permute-start(bf16[256,768]{1,0:T(8,128)(2,1)S(1)} %copy-done.2), channel_id=1, source_target_pairs={{0,1},{1,2},{2,3},{3,4},{4,5},{5,6},{6,7},{7,0},{8,15},{9,8},{10,9... | collective-permute-start | bytes 1179656 | tf_op jit(solution)/shard_map/x1/ppermute | solution.py:102
  25.6 1.6 %copy-start.8 = (f32[32,1024]{1,0:T(8,128)S(1)}, f32[32,1024]{1,0:T(8,128)}, u32[]{:S(2)}) copy-start(f32[32,1024]{1,0:T(8,128)} %get-tuple-element.17) | copy-start | bytes 393220
  28.1 13.1 %all-to-all-start.1 = ((bf16[8,32,1024]{2,1,0:T(8,128)(2,1)}), bf16[8,32,1024]{2,1,0:T(8,128)(2,1)S(1)}, u32[]{:S(2)}, u32[]{:S(2)}) async-start(bf16[8,32,1024]{2,1,0:T(8,128)(2,1)} %broadcast_in_dim.6), calls=%async_computation.1 | async-start | bytes 1048576 | tf_op jit(solution)/shard_map/hidden_spread/all_to_all | solution.py:110
  33.4 5.4 %copy-start.3 = (bf16[256,768]{1,0:T(8,128)(2,1)}, bf16[256,768]{1,0:T(8,128)(2,1)S(1)}, u32[]{:S(2)}) copy-start(bf16[256,768]{1,0:T(8,128)(2,1)S(1)} %collective-permute-done.x1) | copy-start | bytes 1179652
  33.4 4.1 %collective-permute-start.1 = (bf16[256,768]{1,0:T(8,128)(2,1)S(1)}, bf16[256,768]{1,0:T(8,128)(2,1)S(1)}, u32[]{:S(2)}, u32[]{:S(2)}) collective-permute-start(bf16[256,768]{1,0:T(8,128)(2,1)S(1)} %collective-permute-done.x1), channel_id=1, source_target_pairs={{0,8},{8,0},{1,9},{9,1},{2,10},{10,2},{3,11},{11,3},{4,12},{12,4},... | collective-permute-start | bytes 1179656 | tf_op jit(solution)/shard_map/z1/ppermute | solution.py:106
  35.4 15.4 %collective-permute-start.3 = (bf16[256,768]{1,0:T(8,128)(2,1)S(1)}, bf16[256,768]{1,0:T(8,128)(2,1)}, u32[]{:S(2)}, u32[]{:S(2)}) collective-permute-start(bf16[256,768]{1,0:T(8,128)(2,1)S(1)} %collective-permute-done.x1), channel_id=1, source_target_pairs={{0,1},{1,2},{2,3},{3,4},{4,5},{5,6},{6,7},{7,0},{8,15},{9,8},{10,9... | collective-permute-start | bytes 1179656 | tf_op jit(solution)/shard_map/x2/ppermute | solution.py:102
  37.6 0.7 copy-start.4
  41.3 13.9 %all-to-all-start.2 = ((bf16[8,32,128]{2,1,0:T(8,128)(2,1)}), bf16[8,32,128]{2,1,0:T(8,128)(2,1)S(1)}, u32[]{:S(2)}, u32[]{:S(2)}) async-start(bf16[8,32,128]{2,1,0:T(8,128)(2,1)} %bitcast_bitcast_fusion), calls=%async_computation.2 | async-start | bytes 131072 | tf_op jit(solution)/shard_map/batch_spread/all_to_all | solution.py:110
  48.8 17.1 %collective-permute-start.2 = (bf16[4,96,256]{2,1,0:T(8,128)(2,1)S(1)}, bf16[4,96,256]{2,1,0:T(8,128)(2,1)}, u32[]{:S(2)}, u32[]{:S(2)}) collective-permute-start(bf16[4,96,256]{2,1,0:T(8,128)(2,1)S(1)} %dynamic-slice_bitcast_fusion), channel_id=1, source_target_pairs={{0,8},{8,0},{1,9},{9,1},{2,10},{10,2},{3,11},{11,3},{4,12},{12,4},... | collective-permute-start | bytes 589832 | tf_op jit(solution)/shard_map/half_swap/ppermute | solution.py:106
  50.7 16.8 %collective-permute-start.4 = (bf16[256,768]{1,0:T(8,128)(2,1)}, bf16[256,768]{1,0:T(8,128)(2,1)S(1)}, u32[]{:S(2)}, u32[]{:S(2)}) collective-permute-start(bf16[256,768]{1,0:T(8,128)(2,1)} %collective-permute-done.3.x2), channel_id=1, source_target_pairs={{0,1},{1,2},{2,3},{3,4},{4,5},{5,6},{6,7},{7,0},{8,15},{9,8},{10,9... | collective-permute-start | bytes 1179656 | tf_op jit(solution)/shard_map/x3/ppermute | solution.py:102
  55.2 0.6 copy-start.7
  58.1 14.7 %all-to-all-start.3 = ((bf16[8,8,32,128]{3,2,1,0:T(8,128)(2,1)}), bf16[8,8,32,128]{3,2,1,0:T(8,128)(2,1)S(1)}, u32[]{:S(2)}, u32[]{:S(2)}) async-start(bf16[8,8,32,128]{3,2,1,0:T(8,128)(2,1)} %broadcast_in_dim.7), calls=%async_computation.3 | async-start | bytes 1048576 | tf_op jit(solution)/shard_map/across_spread/all_to_all | solution.py:110
  63.5 19.0 %collective-permute-start.6 = (bf16[256,768]{1,0:T(8,128)(2,1)}, bf16[256,768]{1,0:T(8,128)(2,1)S(1)}, u32[]{:S(2)}, u32[]{:S(2)}) collective-permute-start(bf16[256,768]{1,0:T(8,128)(2,1)} %collective-permute-done.3.x2), channel_id=1, source_target_pairs={{0,8},{8,0},{1,9},{9,1},{2,10},{10,2},{3,11},{11,3},{4,12},{12,4},... | collective-permute-start | bytes 1179656 | tf_op jit(solution)/shard_map/z2/ppermute | solution.py:106
  67.6 4.7 %copy-start.5 = (bf16[256,768]{1,0:T(8,128)(2,1)}, bf16[256,768]{1,0:T(8,128)(2,1)S(1)}, u32[]{:S(2)}) copy-start(bf16[256,768]{1,0:T(8,128)(2,1)S(1)} %collective-permute-done.4.refs_0_.x3) | copy-start | bytes 1179652
  67.6 15.0 %collective-permute-start.7 = (bf16[256,768]{1,0:T(8,128)(2,1)S(1)}, bf16[256,768]{1,0:T(8,128)(2,1)}, u32[]{:S(2)}, u32[]{:S(2)}) collective-permute-start(bf16[256,768]{1,0:T(8,128)(2,1)S(1)} %collective-permute-done.4.refs_0_.x3), channel_id=1, source_target_pairs={{0,8},{8,0},{1,9},{9,1},{2,10},{10,2},{3,11},{11,3},{4,12},{12,4},... | collective-permute-start | bytes 1179656 | tf_op jit(solution)/shard_map/z3/ppermute | solution.py:106
  69.5 13.0 %collective-permute-start.5 = (bf16[256,768]{1,0:T(8,128)(2,1)S(1)}, bf16[256,768]{1,0:T(8,128)(2,1)}, u32[]{:S(2)}, u32[]{:S(2)}) collective-permute-start(bf16[256,768]{1,0:T(8,128)(2,1)S(1)} %collective-permute-done.4.refs_0_.x3), channel_id=1, source_target_pairs={{0,1},{1,2},{2,3},{3,4},{4,5},{5,6},{6,7},{7,0},{8,15},{9,8},{10,9... | collective-permute-start | bytes 1179656 | tf_op jit(solution)/shard_map/x4/ppermute | solution.py:102
  72.9 9.7 %copy-start.1 = (bf16[8,8,32,128]{3,2,1,0:T(8,128)(2,1)}, bf16[8,8,32,128]{3,2,1,0:T(8,128)(2,1)S(1)}, u32[]{:S(2)}) copy-start(bf16[8,8,32,128]{3,2,1,0:T(8,128)(2,1)S(1)} %all-to-all-done.3) | copy-start | bytes 1572868
  72.9 20.3 %all-to-all-start.4 = ((bf16[4,96,256]{2,1,0:T(8,128)(2,1)}), bf16[4,96,256]{2,1,0:T(8,128)(2,1)S(1)}, u32[]{:S(2)}, u32[]{:S(2)}) async-start(bf16[4,96,256]{2,1,0:T(8,128)(2,1)} %fusion.1), calls=%async_computation.4 | async-start | bytes 393216 | tf_op jit(solution)/shard_map/zhi_spread/all_to_all | solution.py:110
  82.5 0.8 copy-start.6
Sparse Core Ops, SparseCore 0:
  25.8 47.1 reduce-scatter.1

commit v4 on v3

--- a/solution.py
+++ b/solution.py
@@ -14,6 +14,7 @@
 OUT = ("zhi", "core")
 SWAP = [(0, 1), (1, 0)]
 N = 8
+RING = [(b, (b + 1) % N) for b in range(N)] + [(N + b, N + (b - 1) % N) for b in range(N)]
 
 
 def sds(shape, dtype=BF):
@@ -46,6 +47,10 @@
     return jnp.dot(a, b, preferred_element_type=F32)
 
 
+def ring_sign():
+    return 1 - 2 * lax.axis_index("core")
+
+
 def out_terms(factor, out_grad, pre, term, deriv, turned):
     v = pre[...].astype(F32)
     act = (v * cdf_of(v)).astype(BF)
@@ -54,10 +59,10 @@
     for k in range(N):
         part = slice(k * width, (k + 1) * width)
         term[part, :] = (dot(turned[part, :], act) * factor).astype(BF)
-    rows = pre.shape[0] // N
     i = lax.axis_index(IN)
-    u = pre[pl.ds(pl.multiple_of(i * rows, rows), rows), :].astype(F32)
-    deriv[...] = cdf_of(u) + u * density_of(u)
+    wide = pre.shape[1] // N
+    u = pre[:, pl.ds(pl.multiple_of(i * wide, wide), wide)].astype(F32)
+    deriv[...] = (cdf_of(u) + u * density_of(u)).T
 
 
 def note(flops, *made):
@@ -74,23 +79,25 @@
     )(*made)
 
 
-def weight_grad(factor, recv, x0, x1, x2, x3, x4, z1, z2, z3, step, step2, step3, out):
+def weight_part(at, last, own, other, *refs):
     y = lax.axis_index("batch")
     s = 1 - 2 * lax.axis_index("core")
-    rows = x0.shape[0] // N
-    total = jnp.zeros((out.shape[1], out.shape[0]), F32)
-    for k, ref in ((0, x0), (-1, x1), (-2, x2), (-3, x3), (4, x4), (1, z1), (2, z2), (3, z3)):
-        at = pl.multiple_of(((y + s * k + N) % N) * rows, rows)
-        block = jnp.concatenate([recv[i, pl.ds(at, rows), :] for i in range(N)], 0)
-        total = total + dot(block.T, ref[...])
-    out[...] = (total * factor).T.astype(BF)
+    first = lax.axis_index("zlo") == 0
+    out = refs[-1]
+    total = refs[len(at)][...] if last else jnp.zeros(out.shape, F32)
+    for k, ref in zip(at, refs):
+        b = (y + s * k + N) % N
+        a, c = own[b], other[b]
+        block = jnp.concatenate([jnp.where(first, a, c), jnp.where(first, c, a)], 1)
+        total = total + dot(block, ref[...])
+    out[...] = (total * last).T.astype(BF) if last else total
 
 
 def per_device(inputs, out_grad, pre_act, w_in, w_out):
     tok, d_in = inputs.shape
     hid = pre_act.shape[1]
     factor = 1.0 / math.sqrt(tok * N)
-    piece, wide, rows = d_in // N, hid // N, tok // N
+    piece, wide = d_in // N, hid // N
     core = lax.axis_index("core")
     scope = jax.named_scope
     fence = lax.optimization_barrier
@@ -110,14 +117,14 @@
             return lax.all_to_all(a, axis, 0, 0, tiled=True)
 
     with scope("partial"):
-        part = lax.dot_general(out_grad, w_out, (((1,), (1,)), ((), ())), preferred_element_type=F32)
-        part = part.astype(BF).reshape(N, rows, hid)
+        part = lax.dot_general(w_out, out_grad, (((1,), (1,)), ((), ())), preferred_element_type=F32)
+        part = part.astype(BF).reshape(N, wide, tok)
     got = spread(part, IN, "hidden_reduce")
     x1 = away(inputs, 1, "x1")
     with scope("out_terms"):
         w_out_term, deriv = call(
             functools.partial(out_terms, factor),
-            [sds((d_in, hid)), sds((rows, hid), F32)],
+            [sds((d_in, hid)), sds((wide, tok), F32)],
             out_grad,
             pre_act,
             scratch=[pltpu.VMEM((d_in, tok), BF)],
@@ -130,47 +137,50 @@
         mine = (total * deriv).astype(BF)
     mine, w_out_term = fence((mine, w_out_term))
     with scope("hidden_copy"):
-        copies = jnp.broadcast_to(mine, (N, rows, hid))
-    pg = spread(copies, IN, "hidden_spread").reshape(tok, hid)
-    with scope("hidden_blocks"):
-        blocks = mine.reshape(rows, N, wide).swapaxes(0, 1)
+        mine = jnp.broadcast_to(mine, (N, wide, tok))
+    pg = spread(mine, IN, "hidden_spread")
     x2 = away(x1, 1, "x2")
     z1 = swap(x1, "z1")
     with scope("step"):
         step = note(3000000000, z1)
-    pg, blocks, step = fence((pg, blocks, step))
-    across = spread(blocks, "batch", "batch_spread")
-
+    pg, step = fence((pg, step))
+    with scope("own_tokens"):
+        cols = lax.dynamic_slice_in_dim(pg, lax.axis_index("zlo") * (tok // 2), tok // 2, 2)
+    cols = spread(cols, "batch", "batch_spread")
     with scope("input_term"):
-        term = lax.dot_general(w_in, pg, (((1,), (1,)), ((), ())), preferred_element_type=F32)
-        term = term.astype(BF).reshape(4, 2, piece, tok)
+        term = lax.dot_general(
+            w_in, pg.reshape(hid, tok), (((1,), (0,)), ((), ())), preferred_element_type=F32
+        ).astype(BF).reshape(4, 2, piece, tok)
     with scope("send_half"):
         far_half = lax.dynamic_index_in_dim(term, 1 - core, 1, False)
     got_half = swap(far_half, "half_swap")
     far_half, x2 = fence((far_half, x2))
-    x3 = away(x2, 1, "x3")
-    z2 = swap(x2, "z2")
+    x3, x4 = away(x2, 1, "x3"), away(x2, 2, "x4")
     with scope("keep_half"):
         near = lax.dynamic_index_in_dim(term, core, 1, False)
         kept = (near.astype(F32) + got_half.astype(F32)).astype(BF)
     with scope("step2"):
-        step2 = note(3000000000, across)
-    across, step2 = fence((across, step2))
-    with scope("across_copy"):
-        copies = jnp.broadcast_to(across, (N, N, rows, wide))
-    recv = spread(copies, IN, "across_spread").reshape(N, tok, wide)
-    x4 = away(x3, 1, "x4")
+        step2 = note(3000000000, cols)
+    cols, kept, step2 = fence((cols, kept, step2))
+    with scope("zlo_swap"):
+        more = lax.ppermute(cols, "zlo", SWAP)
+    quad = spread(kept, "zhi", "zhi_spread")
+    z2 = swap(x2, "z2")
+    more, x3 = fence((more, x3))
     z3 = swap(x3, "z3")
-    with scope("step3"):
-        step3 = note(6000000000, x3)
-    recv, kept, step3 = fence((recv, kept, step3))
-    quad = spread(kept, "zhi", "zhi_spread")
     with scope("weight_grad"):
+        early = call(
+            functools.partial(weight_part, (0, -1, -2, 1, 2), 0.0),
+            sds((wide, d_in), F32),
+            cols, more, inputs, x1, x2, z1, z2, step, step2,
+            flops=6000000000,
+            hold=2,
+        )
         w_in_grad = call(
-            functools.partial(weight_grad, factor),
+            functools.partial(weight_part, (-3, 4, 3), factor),
             sds((d_in, wide)),
-            recv, inputs, x1, x2, x3, x4, z1, z2, z3, step, step2, step3,
-            hold=3,
+            cols, more, x3, x4, z3, early,
+            hold=0,
         )
     quad, w_in_grad = fence((quad, w_in_grad))
     with scope("sum_four"):

time: 102 us -> 100 us (0.980)
  the two profiles are of different devices: /device:TPU:2 before, /device:TPU:1 now
where the time goes in v4:
time: 100 us; the launch traced here: 99.3 us
  starting transfers between devices  60.3 us (60%)
  between operations  14.3 us (14%)
  Pallas kernels  11.1 us (11%)
  local copies, waits for them, and re-layouts  7.68 us (8%)
  matrix products  4.45 us (4%)
  other arithmetic  1.46 us (1%)
    all_to_all x4, starting transfers between devices, spread(): return lax.all_to_all(a, axis, 0, 0, tiled=True)  25 us
    ppermute x4, starting transfers between devices, away(): return lax.ppermute(a, ('core', 'batch'), pairs)  18.4 us
    ppermute x4, starting transfers between devices, swap(): return lax.ppermute(a, 'core', SWAP)  14.4 us
    pallas_call x3, Pallas kernels, call(): pl.pallas_call(body, out_shape=outs, in_specs=[vm] * (len(args) - hold) +...  10 us
    unnamed x20, local copies, waits for them, and re-layouts  5.88 us
    ppermute x1, starting transfers between devices, per_device(): more = lax.ppermute(cols, 'zlo', SWAP)  2.46 us
    dot_general x1, matrix products, per_device(): lax.dot_general(w_out, out_grad, (((1,), (1,)), ((), ())), preferred_elem...  2.41 us
    dot_general x1, matrix products, per_device(): lax.dot_general(w_in, pg.reshape(hid, tok), (((1,), (0,)), ((), ())), pre...  2.04 us
  transfers between devices with their start and end apart: 14, of which 0 were waited for; matrix products, arithmetic and copies ran while one was open for 5% of the time, Pallas kernels for 11%

profile of v4, /device:TPU:1, one launch (start us, length us, event | category | flops | bytes accessed | tf_op | source)
XLA Modules:
  0.0 99.3 jit_solution(5082306635675862257)
XLA Ops:
  7.2 1.4 %copy-done = bf16[1024,768]{1,0:T(8,128)(2,1)S(1)} copy-done((bf16[1024,768]{1,0:T(8,128)(2,1)S(1)}, bf16[1024,768]{1,0:T(8,128)(2,1)}, u32[]{:S(2)}) %copy-start) | copy-done | bytes 1572888
  8.6 2.4 %convolution_convert_fusion = bf16[1024,256]{1,0:T(8,128)(2,1)} fusion(bf16[1024,768]{1,0:T(8,128)(2,1)S(1)} %copy-done, bf16[256,768]{1,0:T(8,128)(2,1)} %out_grad.1), kind=kOutput, calls=%fused_computation | convolution fusion | flops 402915328 | bytes 2490368 | tf_op jit(solution)/shard_map/partial/dot_general | solution.py:120
  11.0 6.7 %all-to-all-start = ((bf16[8,128,256]{2,1,0:T(8,128)(2,1)}), bf16[8,128,256]{2,1,0:T(8,128)(2,1)S(1)}, u32[]{:S(2)}, u32[]{:S(2)}) async-start(bf16[8,128,256]{2,1,0:T(8,128)(2,1)} %bitcast), calls=%async_computation | async-start | bytes 1048576 | tf_op jit(solution)/shard_map/hidden_reduce/all_to_all | solution.py:117
  17.7 5.1 %collective-permute-start = (bf16[256,768]{1,0:T(8,128)(2,1)S(1)}, bf16[256,768]{1,0:T(8,128)(2,1)}, u32[]{:S(2)}, u32[]{:S(2)}) collective-permute-start(bf16[256,768]{1,0:T(8,128)(2,1)S(1)} %copy-done.7), channel_id=1, source_target_pairs={{0,1},{1,2},{2,3},{3,4},{4,5},{5,6},{6,7},{7,0},{8,15},{9,8},{10,9... | collective-permute-start | bytes 1179656 | tf_op jit(solution)/shard_map/x1/ppermute | solution.py:109
  22.8 3.3 %out_terms.1 = (bf16[768,1024]{1,0:T(8,128)(2,1)}, f32[128,256]{1,0:T(8,128)}) custom-call(bf16[256,768]{1,0:T(8,128)(2,1)} %out_grad.1, bf16[256,1024]{1,0:T(8,128)(2,1)} %pre.1), custom_call_target="tpu_custom_call" | custom-call | tf_op jit(solution)/shard_map/out_terms/pallas_call | solution.py:27
  26.3 0.8 copy-done.6
  27.1 0.8 broadcast_in_dim.3
  27.9 5.1 %all-to-all-start.1 = ((bf16[8,128,256]{2,1,0:T(8,128)(2,1)}), bf16[8,128,256]{2,1,0:T(8,128)(2,1)S(1)}, u32[]{:S(2)}, u32[]{:S(2)}) async-start(bf16[8,128,256]{2,1,0:T(8,128)(2,1)} %broadcast_in_dim.3), calls=%async_computation.1 | async-start | bytes 1048576 | tf_op jit(solution)/shard_map/hidden_spread/all_to_all | solution.py:117
  33.0 3.3 %collective-permute-start.1 = (bf16[256,768]{1,0:T(8,128)(2,1)}, bf16[256,768]{1,0:T(8,128)(2,1)S(1)}, u32[]{:S(2)}, u32[]{:S(2)}) collective-permute-start(bf16[256,768]{1,0:T(8,128)(2,1)} %collective-permute-done.refs_1_), channel_id=1, source_target_pairs={{0,8},{8,0},{1,9},{9,1},{2,10},{10,2},{3,11},{11,3},{4,12},{12,4},... | collective-permute-start | bytes 1179656 | tf_op jit(solution)/shard_map/z1/ppermute | solution.py:113
  36.4 4.4 %collective-permute-start.4 = (bf16[256,768]{1,0:T(8,128)(2,1)}, bf16[256,768]{1,0:T(8,128)(2,1)}, u32[]{:S(2)}, u32[]{:S(2)}) collective-permute-start(bf16[256,768]{1,0:T(8,128)(2,1)} %collective-permute-done.refs_1_), channel_id=1, source_target_pairs={{0,1},{1,2},{2,3},{3,4},{4,5},{5,6},{6,7},{7,0},{8,15},{9,8},{10,9... | collective-permute-start | bytes 1179656 | tf_op jit(solution)/shard_map/x2/ppermute | solution.py:109
  40.8 0.7 copy-done.8
  41.6 0.5 step.1.refs_5_
  42.1 0.8 constant_dynamic-slice_fusion
  42.9 4.1 %all-to-all-start.2 = ((bf16[8,128,128]{2,1,0:T(8,128)(2,1)}), bf16[8,128,128]{2,1,0:T(8,128)(2,1)S(1)}, u32[]{:S(2)}, u32[]{:S(2)}) async-start(bf16[8,128,128]{2,1,0:T(8,128)(2,1)} %constant_dynamic-slice_fusion), calls=%async_computation.2 | async-start | bytes 524288 | tf_op jit(solution)/shard_map/batch_spread/all_to_all | solution.py:117
  47.0 2.0 %fusion = bf16[768,256]{0,1:T(8,128)(2,1)S(1)} fusion(bf16[1024,256]{1,0:T(8,128)(2,1)S(1)} %bitcast.18, bf16[768,1024]{1,0:T(8,128)(2,1)} %param.8), kind=kOutput, calls=%fused_computation.2 | convolution fusion | flops 402849792 | bytes 2490368 | tf_op jit(solution)/shard_map/input_term/dot_general | solution.py:151
  49.1 0.2 copy.8
  49.3 5.0 %collective-permute-start.2 = (bf16[4,96,256]{2,1,0:T(8,128)(2,1)S(1)}, bf16[4,96,256]{2,1,0:T(8,128)(2,1)S(1)}, u32[]{:S(2)}, u32[]{:S(2)}) collective-permute-start(bf16[4,96,256]{2,1,0:T(8,128)(2,1)S(1)} %dynamic-slice_bitcast_fusion), channel_id=1, source_target_pairs={{0,8},{8,0},{1,9},{9,1},{2,10},{10,2},{3,11},{11,3},{4,12},{12,4},... | collective-permute-start | bytes 589832 | tf_op jit(solution)/shard_map/half_swap/ppermute | solution.py:113
  54.3 1.9 %collective-permute-start.8 = (bf16[256,768]{1,0:T(8,128)(2,1)}, bf16[256,768]{1,0:T(8,128)(2,1)S(1)}, u32[]{:S(2)}, u32[]{:S(2)}) collective-permute-start(bf16[256,768]{1,0:T(8,128)(2,1)} %collective-permute-done.4.refs_2_), channel_id=1, source_target_pairs={{0,8},{8,0},{1,9},{9,1},{2,10},{10,2},{3,11},{11,3},{4,12},{12,4},... | collective-permute-start | bytes 1179656 | tf_op jit(solution)/shard_map/z2/ppermute | solution.py:113
  56.2 4.9 %collective-permute-start.5 = (bf16[256,768]{1,0:T(8,128)(2,1)}, bf16[256,768]{1,0:T(8,128)(2,1)S(1)}, u32[]{:S(2)}, u32[]{:S(2)}) collective-permute-start(bf16[256,768]{1,0:T(8,128)(2,1)} %collective-permute-done.4.refs_2_), channel_id=1, source_target_pairs={{0,1},{1,2},{2,3},{3,4},{4,5},{5,6},{6,7},{7,0},{8,15},{9,8},{10,9... | collective-permute-start | bytes 1179656 | tf_op jit(solution)/shard_map/x3/ppermute | solution.py:109
  61.1 0.7 fusion.1
  61.8 0.7 copy-done.1
  62.5 0.5 step2.1.refs_6_
  63.0 2.5 %collective-permute-start.3 = (bf16[8,128,128]{2,1,0:T(8,128)(2,1)}, bf16[8,128,128]{2,1,0:T(8,128)(2,1)S(1)}, u32[]{:S(2)}, u32[]{:S(2)}) collective-permute-start(bf16[8,128,128]{2,1,0:T(8,128)(2,1)} %copy-done.1), channel_id=1, source_target_pairs={{0,64},{64,0},{1,65},{65,1},{2,66},{66,2},{3,67},{67,3},{4,68},{68... | collective-permute-start | bytes 786440 | tf_op jit(solution)/shard_map/zlo_swap/ppermute | solution.py:166
  65.5 4.0 %collective-permute-start.6 = (bf16[256,768]{1,0:T(8,128)(2,1)}, bf16[256,768]{1,0:T(8,128)(2,1)S(1)}, u32[]{:S(2)}, u32[]{:S(2)}) collective-permute-start(bf16[256,768]{1,0:T(8,128)(2,1)} %collective-permute-done.4.refs_2_), channel_id=1, source_target_pairs={{0,2},{1,3},{2,4},{3,5},{4,6},{5,7},{6,0},{7,1},{8,14},{9,15},{10,... | collective-permute-start | bytes 1179656 | tf_op jit(solution)/shard_map/x4/ppermute | solution.py:109
  69.5 9.1 %all-to-all-start.3 = ((bf16[4,96,256]{2,1,0:T(8,128)(2,1)}), bf16[4,96,256]{2,1,0:T(8,128)(2,1)S(1)}, u32[]{:S(2)}, u32[]{:S(2)}) async-start(bf16[4,96,256]{2,1,0:T(8,128)(2,1)} %fusion.1), calls=%async_computation.3 | async-start | bytes 393216 | tf_op jit(solution)/shard_map/zhi_spread/all_to_all | solution.py:117
  78.7 4.1 %collective-permute-start.7 = (bf16[256,768]{1,0:T(8,128)(2,1)S(1)}, bf16[256,768]{1,0:T(8,128)(2,1)S(1)}, u32[]{:S(2)}, u32[]{:S(2)}) collective-permute-start(bf16[256,768]{1,0:T(8,128)(2,1)S(1)} %collective-permute-done.5.refs_0_), channel_id=1, source_target_pairs={{0,8},{8,0},{1,9},{9,1},{2,10},{10,2},{3,11},{11,3},{4,12},{12,4},... | collective-permute-start | bytes 1179656 | tf_op jit(solution)/shard_map/z3/ppermute | solution.py:113
  82.9 0.7 copy-done.9
  83.6 4.1 %weight_grad.2.refs_3_ = f32[128,768]{1,0:T(8,128)} custom-call(bf16[8,128,128]{2,1,0:T(8,128)(2,1)} %copy-done.1, bf16[8,128,128]{2,1,0:T(8,128)(2,1)} %copy-done.5, bf16[256,768]{1,0:T(8,128)(2,1)} %refs_0_.1, bf16[256,768]{1,0:T(8,128)(2,1)} %collective-permute-done.refs_1_, bf16[256,768]{1,0:T(8,128)(2,1)} %collective-permute-done.4.refs_2_, ...), custom_call_target="tpu_custom_call" | custom-call | flops 6000000000 | tf_op jit(solution)/shard_map/weight_grad/pallas_call | solution.py:27
  87.7 0.7 copy-done.3
  88.5 0.7 copy-done.4
  89.2 2.6 %weight_grad.3 = bf16[768,128]{1,0:T(8,128)(2,1)} custom-call(bf16[8,128,128]{2,1,0:T(8,128)(2,1)} %copy-done.1, bf16[8,128,128]{2,1,0:T(8,128)(2,1)} %copy-done.5, bf16[256,768]{1,0:T(8,128)(2,1)} %copy-done.2, bf16[256,768]{1,0:T(8,128)(2,1)} %copy-done.3, bf16[256,768]{1,0:T(8,128)(2,1)} %copy-done.4, f32[128,768]{1,0:T(8,128)} %weight_grad.2.refs_3_), custom_call_target="tpu_custom_call" | custom-call | tf_op jit(solution)/shard_map/weight_grad/pallas_call | solution.py:27
  91.8 0.7 reduce_sum.22
  (32 shorter events, 0.2 us)
Async XLA Ops:
  7.2 1.4 %copy-start = (bf16[1024,768]{1,0:T(8,128)(2,1)S(1)}, bf16[1024,768]{1,0:T(8,128)(2,1)}, u32[]{:S(2)}) copy-start(bf16[1024,768]{1,0:T(8,128)(2,1)} %param.9) | copy-start | bytes 4718596
  7.2 10.5 %copy-start.7 = (bf16[256,768]{1,0:T(8,128)(2,1)S(1)}, bf16[256,768]{1,0:T(8,128)(2,1)}, u32[]{:S(2)}) copy-start(bf16[256,768]{1,0:T(8,128)(2,1)} %refs_0_.1) | copy-start | bytes 1179652
  11.0 15.2 %all-to-all-start = ((bf16[8,128,256]{2,1,0:T(8,128)(2,1)}), bf16[8,128,256]{2,1,0:T(8,128)(2,1)S(1)}, u32[]{:S(2)}, u32[]{:S(2)}) async-start(bf16[8,128,256]{2,1,0:T(8,128)(2,1)} %bitcast), calls=%async_computation | async-start | bytes 1048576 | tf_op jit(solution)/shard_map/hidden_reduce/all_to_all | solution.py:117
  17.6 74.8 %reduce-scatter.2.cloned.1.call-start = ((), (), s32[]{:S(2)}) async-start(), calls=%async_computation.5 | async-start | bytes 1769472 | tf_op jit(solution)/shard_map/w_out_sum/reduce_scatter | solution.py:133
  17.7 15.3 %collective-permute-start = (bf16[256,768]{1,0:T(8,128)(2,1)S(1)}, bf16[256,768]{1,0:T(8,128)(2,1)}, u32[]{:S(2)}, u32[]{:S(2)}) collective-permute-start(bf16[256,768]{1,0:T(8,128)(2,1)S(1)} %copy-done.7), channel_id=1, source_target_pairs={{0,1},{1,2},{2,3},{3,4},{4,5},{5,6},{6,7},{7,0},{8,15},{9,8},{10,9... | collective-permute-start | bytes 1179656 | tf_op jit(solution)/shard_map/x1/ppermute | solution.py:109
  26.1 0.9 copy-start.6
  27.9 14.2 %all-to-all-start.1 = ((bf16[8,128,256]{2,1,0:T(8,128)(2,1)}), bf16[8,128,256]{2,1,0:T(8,128)(2,1)S(1)}, u32[]{:S(2)}, u32[]{:S(2)}) async-start(bf16[8,128,256]{2,1,0:T(8,128)(2,1)} %broadcast_in_dim.3), calls=%async_computation.1 | async-start | bytes 1048576 | tf_op jit(solution)/shard_map/hidden_spread/all_to_all | solution.py:117
  33.0 7.8 %collective-permute-start.1 = (bf16[256,768]{1,0:T(8,128)(2,1)}, bf16[256,768]{1,0:T(8,128)(2,1)S(1)}, u32[]{:S(2)}, u32[]{:S(2)}) collective-permute-start(bf16[256,768]{1,0:T(8,128)(2,1)} %collective-permute-done.refs_1_), channel_id=1, source_target_pairs={{0,8},{8,0},{1,9},{9,1},{2,10},{10,2},{3,11},{11,3},{4,12},{12,4},... | collective-permute-start | bytes 1179656 | tf_op jit(solution)/shard_map/z1/ppermute | solution.py:113
  36.4 17.9 %collective-permute-start.4 = (bf16[256,768]{1,0:T(8,128)(2,1)}, bf16[256,768]{1,0:T(8,128)(2,1)}, u32[]{:S(2)}, u32[]{:S(2)}) collective-permute-start(bf16[256,768]{1,0:T(8,128)(2,1)} %collective-permute-done.refs_1_), channel_id=1, source_target_pairs={{0,1},{1,2},{2,3},{3,4},{4,5},{5,6},{6,7},{7,0},{8,15},{9,8},{10,9... | collective-permute-start | bytes 1179656 | tf_op jit(solution)/shard_map/x2/ppermute | solution.py:109
  40.8 0.8 copy-start.8
  42.9 18.9 %all-to-all-start.2 = ((bf16[8,128,128]{2,1,0:T(8,128)(2,1)}), bf16[8,128,128]{2,1,0:T(8,128)(2,1)S(1)}, u32[]{:S(2)}, u32[]{:S(2)}) async-start(bf16[8,128,128]{2,1,0:T(8,128)(2,1)} %constant_dynamic-slice_fusion), calls=%async_computation.2 | async-start | bytes 524288 | tf_op jit(solution)/shard_map/batch_spread/all_to_all | solution.py:117
  49.3 11.8 %collective-permute-start.2 = (bf16[4,96,256]{2,1,0:T(8,128)(2,1)S(1)}, bf16[4,96,256]{2,1,0:T(8,128)(2,1)S(1)}, u32[]{:S(2)}, u32[]{:S(2)}) collective-permute-start(bf16[4,96,256]{2,1,0:T(8,128)(2,1)S(1)} %dynamic-slice_bitcast_fusion), channel_id=1, source_target_pairs={{0,8},{8,0},{1,9},{9,1},{2,10},{10,2},{3,11},{11,3},{4,12},{12,4},... | collective-permute-start | bytes 589832 | tf_op jit(solution)/shard_map/half_swap/ppermute | solution.py:113
  54.3 28.6 %collective-permute-start.8 = (bf16[256,768]{1,0:T(8,128)(2,1)}, bf16[256,768]{1,0:T(8,128)(2,1)S(1)}, u32[]{:S(2)}, u32[]{:S(2)}) collective-permute-start(bf16[256,768]{1,0:T(8,128)(2,1)} %collective-permute-done.4.refs_2_), channel_id=1, source_target_pairs={{0,8},{8,0},{1,9},{9,1},{2,10},{10,2},{3,11},{11,3},{4,12},{12,4},... | collective-permute-start | bytes 1179656 | tf_op jit(solution)/shard_map/z2/ppermute | solution.py:113
  56.2 22.4 %collective-permute-start.5 = (bf16[256,768]{1,0:T(8,128)(2,1)}, bf16[256,768]{1,0:T(8,128)(2,1)S(1)}, u32[]{:S(2)}, u32[]{:S(2)}) collective-permute-start(bf16[256,768]{1,0:T(8,128)(2,1)} %collective-permute-done.4.refs_2_), channel_id=1, source_target_pairs={{0,1},{1,2},{2,3},{3,4},{4,5},{5,6},{6,7},{7,0},{8,15},{9,8},{10,9... | collective-permute-start | bytes 1179656 | tf_op jit(solution)/shard_map/x3/ppermute | solution.py:109
  61.8 0.7 copy-start.1
  63.0 15.6 %collective-permute-start.3 = (bf16[8,128,128]{2,1,0:T(8,128)(2,1)}, bf16[8,128,128]{2,1,0:T(8,128)(2,1)S(1)}, u32[]{:S(2)}, u32[]{:S(2)}) collective-permute-start(bf16[8,128,128]{2,1,0:T(8,128)(2,1)} %copy-done.1), channel_id=1, source_target_pairs={{0,64},{64,0},{1,65},{65,1},{2,66},{66,2},{3,67},{67,3},{4,68},{68... | collective-permute-start | bytes 786440 | tf_op jit(solution)/shard_map/zlo_swap/ppermute | solution.py:166
  65.5 22.2 %collective-permute-start.6 = (bf16[256,768]{1,0:T(8,128)(2,1)}, bf16[256,768]{1,0:T(8,128)(2,1)S(1)}, u32[]{:S(2)}, u32[]{:S(2)}) collective-permute-start(bf16[256,768]{1,0:T(8,128)(2,1)} %collective-permute-done.4.refs_2_), channel_id=1, source_target_pairs={{0,2},{1,3},{2,4},{3,5},{4,6},{5,7},{6,0},{7,1},{8,14},{9,15},{10,... | collective-permute-start | bytes 1179656 | tf_op jit(solution)/shard_map/x4/ppermute | solution.py:109
  69.5 22.3 %all-to-all-start.3 = ((bf16[4,96,256]{2,1,0:T(8,128)(2,1)}), bf16[4,96,256]{2,1,0:T(8,128)(2,1)S(1)}, u32[]{:S(2)}, u32[]{:S(2)}) async-start(bf16[4,96,256]{2,1,0:T(8,128)(2,1)} %fusion.1), calls=%async_computation.3 | async-start | bytes 393216 | tf_op jit(solution)/shard_map/zhi_spread/all_to_all | solution.py:117
  78.7 9.0 %copy-start.2 = (bf16[256,768]{1,0:T(8,128)(2,1)}, bf16[256,768]{1,0:T(8,128)(2,1)S(1)}, u32[]{:S(2)}) copy-start(bf16[256,768]{1,0:T(8,128)(2,1)S(1)} %collective-permute-done.5.refs_0_) | copy-start | bytes 1179652
  78.7 4.2 %copy-start.5 = (bf16[8,128,128]{2,1,0:T(8,128)(2,1)}, bf16[8,128,128]{2,1,0:T(8,128)(2,1)S(1)}, u32[]{:S(2)}) copy-start(bf16[8,128,128]{2,1,0:T(8,128)(2,1)S(1)} %collective-permute-done.3.other) | copy-start | bytes 786436
  78.7 9.0 %collective-permute-start.7 = (bf16[256,768]{1,0:T(8,128)(2,1)S(1)}, bf16[256,768]{1,0:T(8,128)(2,1)S(1)}, u32[]{:S(2)}, u32[]{:S(2)}) collective-permute-start(bf16[256,768]{1,0:T(8,128)(2,1)S(1)} %collective-permute-done.5.refs_0_), channel_id=1, source_target_pairs={{0,8},{8,0},{1,9},{9,1},{2,10},{10,2},{3,11},{11,3},{4,12},{12,4},... | collective-permute-start | bytes 1179656 | tf_op jit(solution)/shard_map/z3/ppermute | solution.py:113
  82.8 0.8 copy-start.9
  87.7 0.8 copy-start.3
  88.4 0.7 copy-start.4
Sparse Core Ops, SparseCore 0:
  26.3 46.9 reduce-scatter.1

commit v5 on v4

--- a/solution.py
+++ b/solution.py
@@ -21,7 +21,7 @@
     return jax.ShapeDtypeStruct(shape, dtype)
 
 
-def call(body, outs, *args, scratch=(), flops=0, touched=0, hold=0):
+def call(body, outs, *args, scratch=(), flops=0, touched=0, hold=0, room=60):
     vm = pl.BlockSpec(memory_space=pltpu.VMEM)
     many = isinstance(outs, (list, tuple))
     return pl.pallas_call(
@@ -30,7 +30,7 @@
         in_specs=[vm] * (len(args) - hold) + [pl.BlockSpec(memory_space=pl.ANY)] * hold,
         out_specs=[vm] * len(outs) if many else vm,
         scratch_shapes=list(scratch),
-        compiler_params=pltpu.CompilerParams(vmem_limit_bytes=60 * 1024 * 1024),
+        compiler_params=pltpu.CompilerParams(vmem_limit_bytes=room * 1024 * 1024),
         cost_estimate=pl.CostEstimate(flops=flops, bytes_accessed=touched, transcendentals=0),
     )(*args)
 
@@ -84,13 +84,13 @@
     s = 1 - 2 * lax.axis_index("core")
     first = lax.axis_index("zlo") == 0
     out = refs[-1]
-    total = refs[len(at)][...] if last else jnp.zeros(out.shape, F32)
+    total = refs[len(at)][...].astype(F32) if last else jnp.zeros(out.shape, F32)
     for k, ref in zip(at, refs):
         b = (y + s * k + N) % N
         a, c = own[b], other[b]
         block = jnp.concatenate([jnp.where(first, a, c), jnp.where(first, c, a)], 1)
         total = total + dot(block, ref[...])
-    out[...] = (total * last).T.astype(BF) if last else total
+    out[...] = (total * last).T.astype(BF) if last else total.astype(BF)
 
 
 def per_device(inputs, out_grad, pre_act, w_in, w_out):
@@ -171,16 +171,17 @@
     with scope("weight_grad"):
         early = call(
             functools.partial(weight_part, (0, -1, -2, 1, 2), 0.0),
-            sds((wide, d_in), F32),
+            sds((wide, d_in)),
             cols, more, inputs, x1, x2, z1, z2, step, step2,
             flops=6000000000,
             hold=2,
+            room=62,
         )
         w_in_grad = call(
             functools.partial(weight_part, (-3, 4, 3), factor),
             sds((d_in, wide)),
             cols, more, x3, x4, z3, early,
-            hold=0,
+            room=62,
         )
     quad, w_in_grad = fence((quad, w_in_grad))
     with scope("sum_four"):

time: 100 us -> 97.8 us (0.978)
  local copies, waits for them, and re-layouts: 7.68 us -> 5.42 us
    unnamed x20 -> x14, local copies, waits for them, and re-layouts: 5.88 us -> 3.67 us
where the time goes in v5:
time: 97.8 us; the launch traced here: 96.9 us
  starting transfers between devices  60.2 us (62%)
  between operations  14.3 us (15%)
  Pallas kernels  10.9 us (11%)
  local copies, waits for them, and re-layouts  5.42 us (6%)
  matrix products  4.47 us (5%)
  other arithmetic  1.48 us (2%)
    all_to_all x4, starting transfers between devices, spread(): return lax.all_to_all(a, axis, 0, 0, tiled=True)  25 us
    ppermute x4, starting transfers between devices, away(): return lax.ppermute(a, ('core', 'batch'), pairs)  18.4 us
    ppermute x4, starting transfers between devices, swap(): return lax.ppermute(a, 'core', SWAP)  14.3 us
    pallas_call x3, Pallas kernels, call(): pl.pallas_call(body, out_shape=outs, in_specs=[vm] * (len(args) - hold) +...  9.91 us
    unnamed x14, local copies, waits for them, and re-layouts  3.67 us
    ppermute x1, starting transfers between devices, per_device(): more = lax.ppermute(cols, 'zlo', SWAP)  2.46 us
    dot_general x1, matrix products, per_device(): lax.dot_general(w_out, out_grad, (((1,), (1,)), ((), ())), preferred_elem...  2.43 us
    dot_general x1, matrix products, per_device(): lax.dot_general(w_in, pg.reshape(hid, tok), (((1,), (0,)), ((), ())), pre...  2.04 us
  transfers between devices with their start and end apart: 14, of which 0 were waited for; matrix products, arithmetic and copies ran while one was open for 5% of the time, Pallas kernels for 11%

profile of v5, /device:TPU:1, one launch (start us, length us, event | category | flops | bytes accessed | tf_op | source)
XLA Modules:
  0.0 96.9 jit_solution(13631238710982789584)
XLA Ops:
  7.2 1.4 %copy-done = bf16[1024,768]{1,0:T(8,128)(2,1)S(1)} copy-done((bf16[1024,768]{1,0:T(8,128)(2,1)S(1)}, bf16[1024,768]{1,0:T(8,128)(2,1)}, u32[]{:S(2)}) %copy-start) | copy-done | bytes 1572888
  8.6 2.4 %convolution_convert_fusion = bf16[1024,256]{1,0:T(8,128)(2,1)} fusion(bf16[1024,768]{1,0:T(8,128)(2,1)S(1)} %copy-done, bf16[256,768]{1,0:T(8,128)(2,1)} %out_grad.1), kind=kOutput, calls=%fused_computation | convolution fusion | flops 402915328 | bytes 2490368 | tf_op jit(solution)/shard_map/partial/dot_general | solution.py:120
  11.0 6.7 %all-to-all-start = ((bf16[8,128,256]{2,1,0:T(8,128)(2,1)}), bf16[8,128,256]{2,1,0:T(8,128)(2,1)S(1)}, u32[]{:S(2)}, u32[]{:S(2)}) async-start(bf16[8,128,256]{2,1,0:T(8,128)(2,1)} %bitcast), calls=%async_computation | async-start | bytes 1048576 | tf_op jit(solution)/shard_map/hidden_reduce/all_to_all | solution.py:117
  17.7 0.0 reduce-scatter.2.cloned.1.call-start
  17.7 5.1 %collective-permute-start = (bf16[256,768]{1,0:T(8,128)(2,1)S(1)}, bf16[256,768]{1,0:T(8,128)(2,1)S(1)}, u32[]{:S(2)}, u32[]{:S(2)}) collective-permute-start(bf16[256,768]{1,0:T(8,128)(2,1)S(1)} %copy-done.4), channel_id=1, source_target_pairs={{0,1},{1,2},{2,3},{3,4},{4,5},{5,6},{6,7},{7,0},{8,15},{9,8},{10,9... | collective-permute-start | bytes 1179656 | tf_op jit(solution)/shard_map/x1/ppermute | solution.py:109
  22.8 3.4 %out_terms.1 = (bf16[768,1024]{1,0:T(8,128)(2,1)}, f32[128,256]{1,0:T(8,128)}) custom-call(bf16[256,768]{1,0:T(8,128)(2,1)} %out_grad.1, bf16[256,1024]{1,0:T(8,128)(2,1)} %pre.1), custom_call_target="tpu_custom_call" | custom-call | tf_op jit(solution)/shard_map/out_terms/pallas_call | solution.py:27
  26.2 0.0 reduce-scatter.2.cloned.1.call-update
  26.2 0.1 convert_reduce_fusion
  26.3 0.8 copy-done.3
  27.1 0.8 broadcast_in_dim.3
  27.9 5.1 %all-to-all-start.1 = ((bf16[8,128,256]{2,1,0:T(8,128)(2,1)}), bf16[8,128,256]{2,1,0:T(8,128)(2,1)S(1)}, u32[]{:S(2)}, u32[]{:S(2)}) async-start(bf16[8,128,256]{2,1,0:T(8,128)(2,1)} %broadcast_in_dim.3), calls=%async_computation.1 | async-start | bytes 1048576 | tf_op jit(solution)/shard_map/hidden_spread/all_to_all | solution.py:117
  33.0 3.3 %collective-permute-start.1 = (bf16[256,768]{1,0:T(8,128)(2,1)S(1)}, bf16[256,768]{1,0:T(8,128)(2,1)S(1)}, u32[]{:S(2)}, u32[]{:S(2)}) collective-permute-start(bf16[256,768]{1,0:T(8,128)(2,1)S(1)} %collective-permute-done.refs_1_), channel_id=1, source_target_pairs={{0,8},{8,0},{1,9},{9,1},{2,10},{10,2},{3,11},{11,3},{4,12},{12,4},... | collective-permute-start | bytes 1179656 | tf_op jit(solution)/shard_map/z1/ppermute | solution.py:113
  36.4 4.5 %collective-permute-start.4 = (bf16[256,768]{1,0:T(8,128)(2,1)S(1)}, bf16[256,768]{1,0:T(8,128)(2,1)}, u32[]{:S(2)}, u32[]{:S(2)}) collective-permute-start(bf16[256,768]{1,0:T(8,128)(2,1)S(1)} %collective-permute-done.refs_1_), channel_id=1, source_target_pairs={{0,1},{1,2},{2,3},{3,4},{4,5},{5,6},{6,7},{7,0},{8,15},{9,8},{10,9... | collective-permute-start | bytes 1179656 | tf_op jit(solution)/shard_map/x2/ppermute | solution.py:109
  40.9 0.7 copy-done.6
  41.6 0.5 step.1.refs_5_
  42.2 0.7 constant_dynamic-slice_fusion
  42.9 4.1 %all-to-all-start.2 = ((bf16[8,128,128]{2,1,0:T(8,128)(2,1)}), bf16[8,128,128]{2,1,0:T(8,128)(2,1)S(1)}, u32[]{:S(2)}, u32[]{:S(2)}) async-start(bf16[8,128,128]{2,1,0:T(8,128)(2,1)} %constant_dynamic-slice_fusion), calls=%async_computation.2 | async-start | bytes 524288 | tf_op jit(solution)/shard_map/batch_spread/all_to_all | solution.py:117
  47.0 2.0 %fusion = bf16[768,256]{0,1:T(8,128)(2,1)S(1)} fusion(bf16[1024,256]{1,0:T(8,128)(2,1)S(1)} %bitcast.18, bf16[768,1024]{1,0:T(8,128)(2,1)} %param.8), kind=kOutput, calls=%fused_computation.2 | convolution fusion | flops 402849792 | bytes 2490368 | tf_op jit(solution)/shard_map/input_term/dot_general | solution.py:151
  49.1 0.2 copy.8
  49.3 4.9 %collective-permute-start.2 = (bf16[4,96,256]{2,1,0:T(8,128)(2,1)S(1)}, bf16[4,96,256]{2,1,0:T(8,128)(2,1)S(1)}, u32[]{:S(2)}, u32[]{:S(2)}) collective-permute-start(bf16[4,96,256]{2,1,0:T(8,128)(2,1)S(1)} %dynamic-slice_bitcast_fusion), channel_id=1, source_target_pairs={{0,8},{8,0},{1,9},{9,1},{2,10},{10,2},{3,11},{11,3},{4,12},{12,4},... | collective-permute-start | bytes 589832 | tf_op jit(solution)/shard_map/half_swap/ppermute | solution.py:113
  54.2 1.9 %collective-permute-start.8 = (bf16[256,768]{1,0:T(8,128)(2,1)}, bf16[256,768]{1,0:T(8,128)(2,1)}, u32[]{:S(2)}, u32[]{:S(2)}) collective-permute-start(bf16[256,768]{1,0:T(8,128)(2,1)} %collective-permute-done.4.refs_2_), channel_id=1, source_target_pairs={{0,8},{8,0},{1,9},{9,1},{2,10},{10,2},{3,11},{11,3},{4,12},{12,4},... | collective-permute-start | bytes 1179656 | tf_op jit(solution)/shard_map/z2/ppermute | solution.py:113
  56.2 4.9 %collective-permute-start.5 = (bf16[256,768]{1,0:T(8,128)(2,1)}, bf16[256,768]{1,0:T(8,128)(2,1)}, u32[]{:S(2)}, u32[]{:S(2)}) collective-permute-start(bf16[256,768]{1,0:T(8,128)(2,1)} %collective-permute-done.4.refs_2_), channel_id=1, source_target_pairs={{0,1},{1,2},{2,3},{3,4},{4,5},{5,6},{6,7},{7,0},{8,15},{9,8},{10,9... | collective-permute-start | bytes 1179656 | tf_op jit(solution)/shard_map/x3/ppermute | solution.py:109
  61.1 0.7 fusion.1
  61.8 0.7 copy-done.1
  62.5 0.5 step2.1.refs_6_
  63.1 2.5 %collective-permute-start.3 = (bf16[8,128,128]{2,1,0:T(8,128)(2,1)}, bf16[8,128,128]{2,1,0:T(8,128)(2,1)S(1)}, u32[]{:S(2)}, u32[]{:S(2)}) collective-permute-start(bf16[8,128,128]{2,1,0:T(8,128)(2,1)} %copy-done.1), channel_id=1, source_target_pairs={{0,64},{64,0},{1,65},{65,1},{2,66},{66,2},{3,67},{67,3},{4,68},{68... | collective-permute-start | bytes 786440 | tf_op jit(solution)/shard_map/zlo_swap/ppermute | solution.py:166
  65.5 4.0 %collective-permute-start.6 = (bf16[256,768]{1,0:T(8,128)(2,1)}, bf16[256,768]{1,0:T(8,128)(2,1)}, u32[]{:S(2)}, u32[]{:S(2)}) collective-permute-start(bf16[256,768]{1,0:T(8,128)(2,1)} %collective-permute-done.4.refs_2_), channel_id=1, source_target_pairs={{0,2},{1,3},{2,4},{3,5},{4,6},{5,7},{6,0},{7,1},{8,14},{9,15},{10,... | collective-permute-start | bytes 1179656 | tf_op jit(solution)/shard_map/x4/ppermute | solution.py:109
  69.5 9.1 %all-to-all-start.3 = ((bf16[4,96,256]{2,1,0:T(8,128)(2,1)}), bf16[4,96,256]{2,1,0:T(8,128)(2,1)S(1)}, u32[]{:S(2)}, u32[]{:S(2)}) async-start(bf16[4,96,256]{2,1,0:T(8,128)(2,1)} %fusion.1), calls=%async_computation.3 | async-start | bytes 393216 | tf_op jit(solution)/shard_map/zhi_spread/all_to_all | solution.py:117
  78.7 4.1 %collective-permute-start.7 = (bf16[256,768]{1,0:T(8,128)(2,1)}, bf16[256,768]{1,0:T(8,128)(2,1)}, u32[]{:S(2)}, u32[]{:S(2)}) collective-permute-start(bf16[256,768]{1,0:T(8,128)(2,1)} %collective-permute-done.5.refs_0_), channel_id=1, source_target_pairs={{0,8},{8,0},{1,9},{9,1},{2,10},{10,2},{3,11},{11,3},{4,12},{12,4},... | collective-permute-start | bytes 1179656 | tf_op jit(solution)/shard_map/z3/ppermute | solution.py:113
  82.8 4.0 %weight_grad.2.refs_3_ = bf16[128,768]{1,0:T(8,128)(2,1)} custom-call(bf16[8,128,128]{2,1,0:T(8,128)(2,1)} %copy-done.1, bf16[8,128,128]{2,1,0:T(8,128)(2,1)} %copy-done.2, bf16[256,768]{1,0:T(8,128)(2,1)} %refs_0_.1, bf16[256,768]{1,0:T(8,128)(2,1)} %copy-done.5, bf16[256,768]{1,0:T(8,128)(2,1)} %collective-permute-done.4.refs_2_, ...), custom_call_target="tpu_custom_call" | custom-call | flops 6000000000 | tf_op jit(solution)/shard_map/weight_grad/pallas_call | solution.py:27
  86.8 2.5 %weight_grad.3 = bf16[768,128]{1,0:T(8,128)(2,1)} custom-call(bf16[8,128,128]{2,1,0:T(8,128)(2,1)} %copy-done.1, bf16[8,128,128]{2,1,0:T(8,128)(2,1)} %copy-done.2, bf16[256,768]{1,0:T(8,128)(2,1)} %collective-permute-done.5.refs_0_, bf16[256,768]{1,0:T(8,128)(2,1)} %collective-permute-done.6.refs_1_, bf16[256,768]{1,0:T(8,128)(2,1)} %collective-permute-done.7.refs_2_, ...), custom_call_target="tpu_custom_call" | custom-call | tf_op jit(solution)/shard_map/weight_grad/pallas_call | solution.py:27
  89.4 0.7 reduce_sum.22
  (26 shorter events, 0.1 us)
Async XLA Ops:
  7.2 1.4 %copy-start = (bf16[1024,768]{1,0:T(8,128)(2,1)S(1)}, bf16[1024,768]{1,0:T(8,128)(2,1)}, u32[]{:S(2)}) copy-start(bf16[1024,768]{1,0:T(8,128)(2,1)} %param.9) | copy-start | bytes 4718596
  7.2 10.5 %copy-start.4 = (bf16[256,768]{1,0:T(8,128)(2,1)S(1)}, bf16[256,768]{1,0:T(8,128)(2,1)}, u32[]{:S(2)}) copy-start(bf16[256,768]{1,0:T(8,128)(2,1)} %refs_0_.1) | copy-start | bytes 1179652
  11.0 15.2 %all-to-all-start = ((bf16[8,128,256]{2,1,0:T(8,128)(2,1)}), bf16[8,128,256]{2,1,0:T(8,128)(2,1)S(1)}, u32[]{:S(2)}, u32[]{:S(2)}) async-start(bf16[8,128,256]{2,1,0:T(8,128)(2,1)} %bitcast), calls=%async_computation | async-start | bytes 1048576 | tf_op jit(solution)/shard_map/hidden_reduce/all_to_all | solution.py:117
  17.7 72.4 %reduce-scatter.2.cloned.1.call-start = ((), (), s32[]{:S(2)}) async-start(), calls=%async_computation.5 | async-start | bytes 1769472 | tf_op jit(solution)/shard_map/w_out_sum/reduce_scatter | solution.py:133
  17.7 15.3 %collective-permute-start = (bf16[256,768]{1,0:T(8,128)(2,1)S(1)}, bf16[256,768]{1,0:T(8,128)(2,1)S(1)}, u32[]{:S(2)}, u32[]{:S(2)}) collective-permute-start(bf16[256,768]{1,0:T(8,128)(2,1)S(1)} %copy-done.4), channel_id=1, source_target_pairs={{0,1},{1,2},{2,3},{3,4},{4,5},{5,6},{6,7},{7,0},{8,15},{9,8},{10,9... | collective-permute-start | bytes 1179656 | tf_op jit(solution)/shard_map/x1/ppermute | solution.py:109
  26.2 0.9 copy-start.3
  27.9 14.2 %all-to-all-start.1 = ((bf16[8,128,256]{2,1,0:T(8,128)(2,1)}), bf16[8,128,256]{2,1,0:T(8,128)(2,1)S(1)}, u32[]{:S(2)}, u32[]{:S(2)}) async-start(bf16[8,128,256]{2,1,0:T(8,128)(2,1)} %broadcast_in_dim.3), calls=%async_computation.1 | async-start | bytes 1048576 | tf_op jit(solution)/shard_map/hidden_spread/all_to_all | solution.py:117
  33.0 9.1 %copy-start.5 = (bf16[256,768]{1,0:T(8,128)(2,1)}, bf16[256,768]{1,0:T(8,128)(2,1)S(1)}, u32[]{:S(2)}) copy-start(bf16[256,768]{1,0:T(8,128)(2,1)S(1)} %collective-permute-done.refs_1_) | copy-start | bytes 1179652
  33.0 7.8 %collective-permute-start.1 = (bf16[256,768]{1,0:T(8,128)(2,1)S(1)}, bf16[256,768]{1,0:T(8,128)(2,1)S(1)}, u32[]{:S(2)}, u32[]{:S(2)}) collective-permute-start(bf16[256,768]{1,0:T(8,128)(2,1)S(1)} %collective-permute-done.refs_1_), channel_id=1, source_target_pairs={{0,8},{8,0},{1,9},{9,1},{2,10},{10,2},{3,11},{11,3},{4,12},{12,4},... | collective-permute-start | bytes 1179656 | tf_op jit(solution)/shard_map/z1/ppermute | solution.py:113
  36.4 17.9 %collective-permute-start.4 = (bf16[256,768]{1,0:T(8,128)(2,1)S(1)}, bf16[256,768]{1,0:T(8,128)(2,1)}, u32[]{:S(2)}, u32[]{:S(2)}) collective-permute-start(bf16[256,768]{1,0:T(8,128)(2,1)S(1)} %collective-permute-done.refs_1_), channel_id=1, source_target_pairs={{0,1},{1,2},{2,3},{3,4},{4,5},{5,6},{6,7},{7,0},{8,15},{9,8},{10,9... | collective-permute-start | bytes 1179656 | tf_op jit(solution)/shard_map/x2/ppermute | solution.py:109
  40.9 0.8 copy-start.6
  42.9 18.9 %all-to-all-start.2 = ((bf16[8,128,128]{2,1,0:T(8,128)(2,1)}), bf16[8,128,128]{2,1,0:T(8,128)(2,1)S(1)}, u32[]{:S(2)}, u32[]{:S(2)}) async-start(bf16[8,128,128]{2,1,0:T(8,128)(2,1)} %constant_dynamic-slice_fusion), calls=%async_computation.2 | async-start | bytes 524288 | tf_op jit(solution)/shard_map/batch_spread/all_to_all | solution.py:117
  49.3 11.8 %collective-permute-start.2 = (bf16[4,96,256]{2,1,0:T(8,128)(2,1)S(1)}, bf16[4,96,256]{2,1,0:T(8,128)(2,1)S(1)}, u32[]{:S(2)}, u32[]{:S(2)}) collective-permute-start(bf16[4,96,256]{2,1,0:T(8,128)(2,1)S(1)} %dynamic-slice_bitcast_fusion), channel_id=1, source_target_pairs={{0,8},{8,0},{1,9},{9,1},{2,10},{10,2},{3,11},{11,3},{4,12},{12,4},... | collective-permute-start | bytes 589832 | tf_op jit(solution)/shard_map/half_swap/ppermute | solution.py:113
  54.2 28.5 %collective-permute-start.8 = (bf16[256,768]{1,0:T(8,128)(2,1)}, bf16[256,768]{1,0:T(8,128)(2,1)}, u32[]{:S(2)}, u32[]{:S(2)}) collective-permute-start(bf16[256,768]{1,0:T(8,128)(2,1)} %collective-permute-done.4.refs_2_), channel_id=1, source_target_pairs={{0,8},{8,0},{1,9},{9,1},{2,10},{10,2},{3,11},{11,3},{4,12},{12,4},... | collective-permute-start | bytes 1179656 | tf_op jit(solution)/shard_map/z2/ppermute | solution.py:113
  56.2 22.5 %collective-permute-start.5 = (bf16[256,768]{1,0:T(8,128)(2,1)}, bf16[256,768]{1,0:T(8,128)(2,1)}, u32[]{:S(2)}, u32[]{:S(2)}) collective-permute-start(bf16[256,768]{1,0:T(8,128)(2,1)} %collective-permute-done.4.refs_2_), channel_id=1, source_target_pairs={{0,1},{1,2},{2,3},{3,4},{4,5},{5,6},{6,7},{7,0},{8,15},{9,8},{10,9... | collective-permute-start | bytes 1179656 | tf_op jit(solution)/shard_map/x3/ppermute | solution.py:109
  61.8 0.7 copy-start.1
  63.1 15.6 %collective-permute-start.3 = (bf16[8,128,128]{2,1,0:T(8,128)(2,1)}, bf16[8,128,128]{2,1,0:T(8,128)(2,1)S(1)}, u32[]{:S(2)}, u32[]{:S(2)}) collective-permute-start(bf16[8,128,128]{2,1,0:T(8,128)(2,1)} %copy-done.1), channel_id=1, source_target_pairs={{0,64},{64,0},{1,65},{65,1},{2,66},{66,2},{3,67},{67,3},{4,68},{68... | collective-permute-start | bytes 786440 | tf_op jit(solution)/shard_map/zlo_swap/ppermute | solution.py:166
  65.5 21.3 %collective-permute-start.6 = (bf16[256,768]{1,0:T(8,128)(2,1)}, bf16[256,768]{1,0:T(8,128)(2,1)}, u32[]{:S(2)}, u32[]{:S(2)}) collective-permute-start(bf16[256,768]{1,0:T(8,128)(2,1)} %collective-permute-done.4.refs_2_), channel_id=1, source_target_pairs={{0,2},{1,3},{2,4},{3,5},{4,6},{5,7},{6,0},{7,1},{8,14},{9,15},{10,... | collective-permute-start | bytes 1179656 | tf_op jit(solution)/shard_map/x4/ppermute | solution.py:109
  69.5 19.8 %all-to-all-start.3 = ((bf16[4,96,256]{2,1,0:T(8,128)(2,1)}), bf16[4,96,256]{2,1,0:T(8,128)(2,1)S(1)}, u32[]{:S(2)}, u32[]{:S(2)}) async-start(bf16[4,96,256]{2,1,0:T(8,128)(2,1)} %fusion.1), calls=%async_computation.3 | async-start | bytes 393216 | tf_op jit(solution)/shard_map/zhi_spread/all_to_all | solution.py:117
  78.7 4.1 %copy-start.2 = (bf16[8,128,128]{2,1,0:T(8,128)(2,1)}, bf16[8,128,128]{2,1,0:T(8,128)(2,1)S(1)}, u32[]{:S(2)}) copy-start(bf16[8,128,128]{2,1,0:T(8,128)(2,1)S(1)} %collective-permute-done.3.other) | copy-start | bytes 786436
  78.7 8.1 %collective-permute-start.7 = (bf16[256,768]{1,0:T(8,128)(2,1)}, bf16[256,768]{1,0:T(8,128)(2,1)}, u32[]{:S(2)}, u32[]{:S(2)}) collective-permute-start(bf16[256,768]{1,0:T(8,128)(2,1)} %collective-permute-done.5.refs_0_), channel_id=1, source_target_pairs={{0,8},{8,0},{1,9},{9,1},{2,10},{10,2},{3,11},{11,3},{4,12},{12,4},... | collective-permute-start | bytes 1179656 | tf_op jit(solution)/shard_map/z3/ppermute | solution.py:113
Sparse Core Ops, SparseCore 0:
  26.3 47.1 reduce-scatter.1

commit v6 on v5

--- a/solution.py
+++ b/solution.py
@@ -74,7 +74,7 @@
         out_shape=sds((1, 1), jnp.int32),
         in_specs=[pl.BlockSpec(memory_space=pl.ANY)] * len(made),
         out_specs=pl.BlockSpec(memory_space=pltpu.SMEM),
-        compiler_params=pltpu.CompilerParams(vmem_limit_bytes=60 * 1024 * 1024),
+        compiler_params=pltpu.CompilerParams(vmem_limit_bytes=16 * 1024 * 1024),
         cost_estimate=pl.CostEstimate(flops=flops, bytes_accessed=0, transcendentals=0),
     )(*made)
 

time: 97.8 us -> 97.6 us (level)
  transfers between devices with their start and end apart: 14 -> 14, of which waited for: 0 -> 1; matrix products, arithmetic and copies ran while one was open for 5% -> 5% of each run, Pallas kernels for 11% -> 11%
where the time goes in v6:
time: 97.6 us; the launch traced here: 96.8 us
  starting transfers between devices  60.3 us (62%)
  between operations  14.3 us (15%)
  Pallas kernels  11 us (11%)
  local copies, waits for them, and re-layouts  5.04 us (5%)
  matrix products  4.47 us (5%)
  other arithmetic  1.48 us (2%)
    all_to_all x4, starting transfers between devices, spread(): return lax.all_to_all(a, axis, 0, 0, tiled=True)  25.4 us
    ppermute x4, starting transfers between devices, away(): return lax.ppermute(a, ('core', 'batch'), pairs)  18.4 us
    ppermute x4, starting transfers between devices, swap(): return lax.ppermute(a, 'core', SWAP)  14 us
    pallas_call x3, Pallas kernels, call(): pl.pallas_call(body, out_shape=outs, in_specs=[vm] * (len(args) - hold) +...  9.91 us
    unnamed x14, local copies, waits for them, and re-layouts  3.3 us
    ppermute x1, starting transfers between devices, per_device(): more = lax.ppermute(cols, 'zlo', SWAP)  2.44 us
    dot_general x1, matrix products, per_device(): lax.dot_general(w_out, out_grad, (((1,), (1,)), ((), ())), preferred_elem...  2.43 us
    dot_general x1, matrix products, per_device(): lax.dot_general(w_in, pg.reshape(hid, tok), (((1,), (0,)), ((), ())), pre...  2.04 us
  transfers between devices with their start and end apart: 14, of which 1 were waited for; matrix products, arithmetic and copies ran while one was open for 5% of the time, Pallas kernels for 11%

profile of v6, /device:TPU:1, one launch (start us, length us, event | category | flops | bytes accessed | tf_op | source)
XLA Modules:
  0.0 96.8 jit_solution(118309649906863134)
XLA Ops:
  7.2 1.4 %copy-done = bf16[1024,768]{1,0:T(8,128)(2,1)S(1)} copy-done((bf16[1024,768]{1,0:T(8,128)(2,1)S(1)}, bf16[1024,768]{1,0:T(8,128)(2,1)}, u32[]{:S(2)}) %copy-start) | copy-done | bytes 1572888
  8.6 2.4 %convolution_convert_fusion = bf16[1024,256]{1,0:T(8,128)(2,1)} fusion(bf16[1024,768]{1,0:T(8,128)(2,1)S(1)} %copy-done, bf16[256,768]{1,0:T(8,128)(2,1)} %out_grad.1), kind=kOutput, calls=%fused_computation | convolution fusion | flops 402915328 | bytes 2490368 | tf_op jit(solution)/shard_map/partial/dot_general | solution.py:120
  11.0 6.7 %all-to-all-start = ((bf16[8,128,256]{2,1,0:T(8,128)(2,1)}), bf16[8,128,256]{2,1,0:T(8,128)(2,1)S(1)}, u32[]{:S(2)}, u32[]{:S(2)}) async-start(bf16[8,128,256]{2,1,0:T(8,128)(2,1)} %bitcast), calls=%async_computation | async-start | bytes 1048576 | tf_op jit(solution)/shard_map/hidden_reduce/all_to_all | solution.py:117
  17.7 5.1 %collective-permute-start = (bf16[256,768]{1,0:T(8,128)(2,1)S(1)}, bf16[256,768]{1,0:T(8,128)(2,1)S(1)}, u32[]{:S(2)}, u32[]{:S(2)}) collective-permute-start(bf16[256,768]{1,0:T(8,128)(2,1)S(1)} %copy-done.5), channel_id=1, source_target_pairs={{0,1},{1,2},{2,3},{3,4},{4,5},{5,6},{6,7},{7,0},{8,15},{9,8},{10,9... | collective-permute-start | bytes 1179656 | tf_op jit(solution)/shard_map/x1/ppermute | solution.py:109
  22.8 3.4 %out_terms.1 = (bf16[768,1024]{1,0:T(8,128)(2,1)}, f32[128,256]{1,0:T(8,128)}) custom-call(bf16[256,768]{1,0:T(8,128)(2,1)} %out_grad.1, bf16[256,1024]{1,0:T(8,128)(2,1)} %pre.1), custom_call_target="tpu_custom_call" | custom-call | tf_op jit(solution)/shard_map/out_terms/pallas_call | solution.py:27
  26.2 0.1 convert_reduce_fusion
  26.3 0.8 copy-done.4
  27.1 0.8 broadcast_in_dim.3
  27.9 5.1 %all-to-all-start.1 = ((bf16[8,128,256]{2,1,0:T(8,128)(2,1)}), bf16[8,128,256]{2,1,0:T(8,128)(2,1)S(1)}, u32[]{:S(2)}, u32[]{:S(2)}) async-start(bf16[8,128,256]{2,1,0:T(8,128)(2,1)} %broadcast_in_dim.3), calls=%async_computation.1 | async-start | bytes 1048576 | tf_op jit(solution)/shard_map/hidden_spread/all_to_all | solution.py:117
  33.0 3.3 %collective-permute-start.1 = (bf16[256,768]{1,0:T(8,128)(2,1)S(1)}, bf16[256,768]{1,0:T(8,128)(2,1)S(1)}, u32[]{:S(2)}, u32[]{:S(2)}) collective-permute-start(bf16[256,768]{1,0:T(8,128)(2,1)S(1)} %collective-permute-done.refs_1_), channel_id=1, source_target_pairs={{0,8},{8,0},{1,9},{9,1},{2,10},{10,2},{3,11},{11,3},{4,12},{12,4},... | collective-permute-start | bytes 1179656 | tf_op jit(solution)/shard_map/z1/ppermute | solution.py:113
  36.4 4.5 %collective-permute-start.4 = (bf16[256,768]{1,0:T(8,128)(2,1)S(1)}, bf16[256,768]{1,0:T(8,128)(2,1)}, u32[]{:S(2)}, u32[]{:S(2)}) collective-permute-start(bf16[256,768]{1,0:T(8,128)(2,1)S(1)} %collective-permute-done.refs_1_), channel_id=1, source_target_pairs={{0,1},{1,2},{2,3},{3,4},{4,5},{5,6},{6,7},{7,0},{8,15},{9,8},{10,9... | collective-permute-start | bytes 1179656 | tf_op jit(solution)/shard_map/x2/ppermute | solution.py:109
  40.9 0.5 step.1.refs_5_
  41.4 0.2 copy-done.2
  41.6 0.2 all-to-all-done.1
  41.8 0.7 constant_dynamic-slice_fusion
  42.5 4.5 %all-to-all-start.2 = ((bf16[8,128,128]{2,1,0:T(8,128)(2,1)}), bf16[8,128,128]{2,1,0:T(8,128)(2,1)S(1)}, u32[]{:S(2)}, u32[]{:S(2)}) async-start(bf16[8,128,128]{2,1,0:T(8,128)(2,1)} %constant_dynamic-slice_fusion), calls=%async_computation.2 | async-start | bytes 524288 | tf_op jit(solution)/shard_map/batch_spread/all_to_all | solution.py:117
  47.0 2.0 %fusion = bf16[768,256]{0,1:T(8,128)(2,1)S(1)} fusion(bf16[1024,256]{1,0:T(8,128)(2,1)S(1)} %bitcast.18, bf16[768,1024]{1,0:T(8,128)(2,1)} %param.8), kind=kOutput, calls=%fused_computation.2 | convolution fusion | flops 402849792 | bytes 2490368 | tf_op jit(solution)/shard_map/input_term/dot_general | solution.py:151
  49.1 0.2 copy.8
  49.3 5.0 %collective-permute-start.2 = (bf16[4,96,256]{2,1,0:T(8,128)(2,1)S(1)}, bf16[4,96,256]{2,1,0:T(8,128)(2,1)S(1)}, u32[]{:S(2)}, u32[]{:S(2)}) collective-permute-start(bf16[4,96,256]{2,1,0:T(8,128)(2,1)S(1)} %dynamic-slice_bitcast_fusion), channel_id=1, source_target_pairs={{0,8},{8,0},{1,9},{9,1},{2,10},{10,2},{3,11},{11,3},{4,12},{12,4},... | collective-permute-start | bytes 589832 | tf_op jit(solution)/shard_map/half_swap/ppermute | solution.py:113
  54.2 1.9 %collective-permute-start.8 = (bf16[256,768]{1,0:T(8,128)(2,1)}, bf16[256,768]{1,0:T(8,128)(2,1)}, u32[]{:S(2)}, u32[]{:S(2)}) collective-permute-start(bf16[256,768]{1,0:T(8,128)(2,1)} %collective-permute-done.4.refs_2_), channel_id=1, source_target_pairs={{0,8},{8,0},{1,9},{9,1},{2,10},{10,2},{3,11},{11,3},{4,12},{12,4},... | collective-permute-start | bytes 1179656 | tf_op jit(solution)/shard_map/z2/ppermute | solution.py:113
  56.2 4.9 %collective-permute-start.5 = (bf16[256,768]{1,0:T(8,128)(2,1)}, bf16[256,768]{1,0:T(8,128)(2,1)}, u32[]{:S(2)}, u32[]{:S(2)}) collective-permute-start(bf16[256,768]{1,0:T(8,128)(2,1)} %collective-permute-done.4.refs_2_), channel_id=1, source_target_pairs={{0,1},{1,2},{2,3},{3,4},{4,5},{5,6},{6,7},{7,0},{8,15},{9,8},{10,9... | collective-permute-start | bytes 1179656 | tf_op jit(solution)/shard_map/x3/ppermute | solution.py:109
  61.1 0.7 fusion.1
  61.8 0.5 step2.1.refs_6_
  62.3 0.2 copy-done.1
  62.5 2.4 %collective-permute-start.3 = (bf16[8,128,128]{2,1,0:T(8,128)(2,1)S(1)}, bf16[8,128,128]{2,1,0:T(8,128)(2,1)S(1)}, u32[]{:S(2)}, u32[]{:S(2)}) collective-permute-start(bf16[8,128,128]{2,1,0:T(8,128)(2,1)S(1)} %all-to-all-done.2.refs_0_.own), channel_id=1, source_target_pairs={{0,64},{64,0},{1,65},{65,1},{2,66},{66,2},{3,67},{67,3},{4,68},{68... | collective-permute-start | bytes 786440 | tf_op jit(solution)/shard_map/zlo_swap/ppermute | solution.py:166
  65.0 4.0 %collective-permute-start.6 = (bf16[256,768]{1,0:T(8,128)(2,1)}, bf16[256,768]{1,0:T(8,128)(2,1)}, u32[]{:S(2)}, u32[]{:S(2)}) collective-permute-start(bf16[256,768]{1,0:T(8,128)(2,1)} %collective-permute-done.4.refs_2_), channel_id=1, source_target_pairs={{0,2},{1,3},{2,4},{3,5},{4,6},{5,7},{6,0},{7,1},{8,14},{9,15},{10,... | collective-permute-start | bytes 1179656 | tf_op jit(solution)/shard_map/x4/ppermute | solution.py:109
  69.0 9.1 %all-to-all-start.3 = ((bf16[4,96,256]{2,1,0:T(8,128)(2,1)}), bf16[4,96,256]{2,1,0:T(8,128)(2,1)S(1)}, u32[]{:S(2)}, u32[]{:S(2)}) async-start(bf16[4,96,256]{2,1,0:T(8,128)(2,1)} %fusion.1), calls=%async_computation.3 | async-start | bytes 393216 | tf_op jit(solution)/shard_map/zhi_spread/all_to_all | solution.py:117
  78.2 0.7 copy-done.3
  78.8 3.8 %collective-permute-start.7 = (bf16[256,768]{1,0:T(8,128)(2,1)}, bf16[256,768]{1,0:T(8,128)(2,1)}, u32[]{:S(2)}, u32[]{:S(2)}) collective-permute-start(bf16[256,768]{1,0:T(8,128)(2,1)} %collective-permute-done.5.refs_0_), channel_id=1, source_target_pairs={{0,8},{8,0},{1,9},{9,1},{2,10},{10,2},{3,11},{11,3},{4,12},{12,4},... | collective-permute-start | bytes 1179656 | tf_op jit(solution)/shard_map/z3/ppermute | solution.py:113
  82.7 4.0 %weight_grad.2.refs_3_ = bf16[128,768]{1,0:T(8,128)(2,1)} custom-call(bf16[8,128,128]{2,1,0:T(8,128)(2,1)} %copy-done.1, bf16[8,128,128]{2,1,0:T(8,128)(2,1)} %copy-done.3, bf16[256,768]{1,0:T(8,128)(2,1)} %refs_0_.1, bf16[256,768]{1,0:T(8,128)(2,1)} %copy-done.6, bf16[256,768]{1,0:T(8,128)(2,1)} %collective-permute-done.4.refs_2_, ...), custom_call_target="tpu_custom_call" | custom-call | flops 6000000000 | tf_op jit(solution)/shard_map/weight_grad/pallas_call | solution.py:27
  86.7 2.5 %weight_grad.3 = bf16[768,128]{1,0:T(8,128)(2,1)} custom-call(bf16[8,128,128]{2,1,0:T(8,128)(2,1)} %copy-done.1, bf16[8,128,128]{2,1,0:T(8,128)(2,1)} %copy-done.3, bf16[256,768]{1,0:T(8,128)(2,1)} %collective-permute-done.5.refs_0_, bf16[256,768]{1,0:T(8,128)(2,1)} %collective-permute-done.6.refs_1_, bf16[256,768]{1,0:T(8,128)(2,1)} %collective-permute-done.7.refs_2_, ...), custom_call_target="tpu_custom_call" | custom-call | tf_op jit(solution)/shard_map/weight_grad/pallas_call | solution.py:27
  89.3 0.7 reduce_sum.22
  (26 shorter events, 0.1 us)
Async XLA Ops:
  7.2 1.4 %copy-start = (bf16[1024,768]{1,0:T(8,128)(2,1)S(1)}, bf16[1024,768]{1,0:T(8,128)(2,1)}, u32[]{:S(2)}) copy-start(bf16[1024,768]{1,0:T(8,128)(2,1)} %param.9) | copy-start | bytes 4718596
  7.2 10.5 %copy-start.5 = (bf16[256,768]{1,0:T(8,128)(2,1)S(1)}, bf16[256,768]{1,0:T(8,128)(2,1)}, u32[]{:S(2)}) copy-start(bf16[256,768]{1,0:T(8,128)(2,1)} %refs_0_.1) | copy-start | bytes 1179652
  11.0 15.2 %all-to-all-start = ((bf16[8,128,256]{2,1,0:T(8,128)(2,1)}), bf16[8,128,256]{2,1,0:T(8,128)(2,1)S(1)}, u32[]{:S(2)}, u32[]{:S(2)}) async-start(bf16[8,128,256]{2,1,0:T(8,128)(2,1)} %bitcast), calls=%async_computation | async-start | bytes 1048576 | tf_op jit(solution)/shard_map/hidden_reduce/all_to_all | solution.py:117
  17.7 72.2 %reduce-scatter.2.cloned.1.call-start = ((), (), s32[]{:S(2)}) async-start(), calls=%async_computation.5 | async-start | bytes 1769472 | tf_op jit(solution)/shard_map/w_out_sum/reduce_scatter | solution.py:133
  17.7 15.3 %collective-permute-start = (bf16[256,768]{1,0:T(8,128)(2,1)S(1)}, bf16[256,768]{1,0:T(8,128)(2,1)S(1)}, u32[]{:S(2)}, u32[]{:S(2)}) collective-permute-start(bf16[256,768]{1,0:T(8,128)(2,1)S(1)} %copy-done.5), channel_id=1, source_target_pairs={{0,1},{1,2},{2,3},{3,4},{4,5},{5,6},{6,7},{7,0},{8,15},{9,8},{10,9... | collective-permute-start | bytes 1179656 | tf_op jit(solution)/shard_map/x1/ppermute | solution.py:109
  26.2 0.9 copy-start.4
  27.9 13.9 %all-to-all-start.1 = ((bf16[8,128,256]{2,1,0:T(8,128)(2,1)}), bf16[8,128,256]{2,1,0:T(8,128)(2,1)S(1)}, u32[]{:S(2)}, u32[]{:S(2)}) async-start(bf16[8,128,256]{2,1,0:T(8,128)(2,1)} %broadcast_in_dim.3), calls=%async_computation.1 | async-start | bytes 1048576 | tf_op jit(solution)/shard_map/hidden_spread/all_to_all | solution.py:117
  33.0 8.4 %copy-start.6 = (bf16[256,768]{1,0:T(8,128)(2,1)}, bf16[256,768]{1,0:T(8,128)(2,1)S(1)}, u32[]{:S(2)}) copy-start(bf16[256,768]{1,0:T(8,128)(2,1)S(1)} %collective-permute-done.refs_1_) | copy-start | bytes 1179652
  33.0 7.8 %collective-permute-start.1 = (bf16[256,768]{1,0:T(8,128)(2,1)S(1)}, bf16[256,768]{1,0:T(8,128)(2,1)S(1)}, u32[]{:S(2)}, u32[]{:S(2)}) collective-permute-start(bf16[256,768]{1,0:T(8,128)(2,1)S(1)} %collective-permute-done.refs_1_), channel_id=1, source_target_pairs={{0,8},{8,0},{1,9},{9,1},{2,10},{10,2},{3,11},{11,3},{4,12},{12,4},... | collective-permute-start | bytes 1179656 | tf_op jit(solution)/shard_map/z1/ppermute | solution.py:113
  36.4 17.9 %collective-permute-start.4 = (bf16[256,768]{1,0:T(8,128)(2,1)S(1)}, bf16[256,768]{1,0:T(8,128)(2,1)}, u32[]{:S(2)}, u32[]{:S(2)}) collective-permute-start(bf16[256,768]{1,0:T(8,128)(2,1)S(1)} %collective-permute-done.refs_1_), channel_id=1, source_target_pairs={{0,1},{1,2},{2,3},{3,4},{4,5},{5,6},{6,7},{7,0},{8,15},{9,8},{10,9... | collective-permute-start | bytes 1179656 | tf_op jit(solution)/shard_map/x2/ppermute | solution.py:109
  40.9 0.8 copy-start.2
  42.5 19.3 %all-to-all-start.2 = ((bf16[8,128,128]{2,1,0:T(8,128)(2,1)}), bf16[8,128,128]{2,1,0:T(8,128)(2,1)S(1)}, u32[]{:S(2)}, u32[]{:S(2)}) async-start(bf16[8,128,128]{2,1,0:T(8,128)(2,1)} %constant_dynamic-slice_fusion), calls=%async_computation.2 | async-start | bytes 524288 | tf_op jit(solution)/shard_map/batch_spread/all_to_all | solution.py:117
  49.3 11.8 %collective-permute-start.2 = (bf16[4,96,256]{2,1,0:T(8,128)(2,1)S(1)}, bf16[4,96,256]{2,1,0:T(8,128)(2,1)S(1)}, u32[]{:S(2)}, u32[]{:S(2)}) collective-permute-start(bf16[4,96,256]{2,1,0:T(8,128)(2,1)S(1)} %dynamic-slice_bitcast_fusion), channel_id=1, source_target_pairs={{0,8},{8,0},{1,9},{9,1},{2,10},{10,2},{3,11},{11,3},{4,12},{12,4},... | collective-permute-start | bytes 589832 | tf_op jit(solution)/shard_map/half_swap/ppermute | solution.py:113
  54.2 28.4 %collective-permute-start.8 = (bf16[256,768]{1,0:T(8,128)(2,1)}, bf16[256,768]{1,0:T(8,128)(2,1)}, u32[]{:S(2)}, u32[]{:S(2)}) collective-permute-start(bf16[256,768]{1,0:T(8,128)(2,1)} %collective-permute-done.4.refs_2_), channel_id=1, source_target_pairs={{0,8},{8,0},{1,9},{9,1},{2,10},{10,2},{3,11},{11,3},{4,12},{12,4},... | collective-permute-start | bytes 1179656 | tf_op jit(solution)/shard_map/z2/ppermute | solution.py:113
  56.2 22.0 %collective-permute-start.5 = (bf16[256,768]{1,0:T(8,128)(2,1)}, bf16[256,768]{1,0:T(8,128)(2,1)}, u32[]{:S(2)}, u32[]{:S(2)}) collective-permute-start(bf16[256,768]{1,0:T(8,128)(2,1)} %collective-permute-done.4.refs_2_), channel_id=1, source_target_pairs={{0,1},{1,2},{2,3},{3,4},{4,5},{5,6},{6,7},{7,0},{8,15},{9,8},{10,9... | collective-permute-start | bytes 1179656 | tf_op jit(solution)/shard_map/x3/ppermute | solution.py:109
  61.8 0.7 copy-start.1
  62.5 15.6 %collective-permute-start.3 = (bf16[8,128,128]{2,1,0:T(8,128)(2,1)S(1)}, bf16[8,128,128]{2,1,0:T(8,128)(2,1)S(1)}, u32[]{:S(2)}, u32[]{:S(2)}) collective-permute-start(bf16[8,128,128]{2,1,0:T(8,128)(2,1)S(1)} %all-to-all-done.2.refs_0_.own), channel_id=1, source_target_pairs={{0,64},{64,0},{1,65},{65,1},{2,66},{66,2},{3,67},{67,3},{4,68},{68... | collective-permute-start | bytes 786440 | tf_op jit(solution)/shard_map/zlo_swap/ppermute | solution.py:166
  65.0 21.7 %collective-permute-start.6 = (bf16[256,768]{1,0:T(8,128)(2,1)}, bf16[256,768]{1,0:T(8,128)(2,1)}, u32[]{:S(2)}, u32[]{:S(2)}) collective-permute-start(bf16[256,768]{1,0:T(8,128)(2,1)} %collective-permute-done.4.refs_2_), channel_id=1, source_target_pairs={{0,2},{1,3},{2,4},{3,5},{4,6},{5,7},{6,0},{7,1},{8,14},{9,15},{10,... | collective-permute-start | bytes 1179656 | tf_op jit(solution)/shard_map/x4/ppermute | solution.py:109
  69.0 20.3 %all-to-all-start.3 = ((bf16[4,96,256]{2,1,0:T(8,128)(2,1)}), bf16[4,96,256]{2,1,0:T(8,128)(2,1)S(1)}, u32[]{:S(2)}, u32[]{:S(2)}) async-start(bf16[4,96,256]{2,1,0:T(8,128)(2,1)} %fusion.1), calls=%async_computation.3 | async-start | bytes 393216 | tf_op jit(solution)/shard_map/zhi_spread/all_to_all | solution.py:117
  78.1 0.7 copy-start.3
  78.8 7.9 %collective-permute-start.7 = (bf16[256,768]{1,0:T(8,128)(2,1)}, bf16[256,768]{1,0:T(8,128)(2,1)}, u32[]{:S(2)}, u32[]{:S(2)}) collective-permute-start(bf16[256,768]{1,0:T(8,128)(2,1)} %collective-permute-done.5.refs_0_), channel_id=1, source_target_pairs={{0,8},{8,0},{1,9},{9,1},{2,10},{10,2},{3,11},{11,3},{4,12},{12,4},... | collective-permute-start | bytes 1179656 | tf_op jit(solution)/shard_map/z3/ppermute | solution.py:113
Sparse Core Ops, SparseCore 0:
  26.3 47.1 reduce-scatter.1
